TPU v7x, 128 devices: a whole 4x4x4 slice. The times are simulated.
128 devices in a mesh: dp: 16 (over z_hi, x, core), vocab: 8 (over z_lo, y).
Axes of the slice: x: 4, y: 4, z: 4 (z_hi: 2, z_lo: 2; z = z_hi * 2 + z_lo), core: 2. Of those that a mesh axis runs over, the one named last changes fastest.
Arguments:
- hidden: bfloat16 [512, 4608], P('dp'), may hold values from -6 to 6
- head: bfloat16 [4608, 131072], P(None, ('dp', 'vocab')), may hold values from -0.1875 to 0.1875
- verdict_ids: int32 [512], replicated, may hold values from 0 to 131071
- row_weight: float32 [512], replicated, may hold values from 0.5 to 2
Outputs:
- logprob: float32 [512], P('dp')
- head_grad: bfloat16 [4608, 131072], P(None, ('dp', 'vocab'))
- hidden_grad: bfloat16 [512, 4608], P('dp', 'vocab')
Inputs may be any that keep to these rules, and one draw needn't show every extreme that they name: `verdict_ids`: each row's verdict token is a column of the whole vocabulary of 131072.
All inputs are finite; a program needn't handle non-finite values.
Results may differ from a plain program's by a relative error of at most 0.02.
Values may be sent and summed in bfloat16 or wider, within the bound.
No kernel may reach another device: no remote copies, remote signals or barrier semaphores. Data moves between devices by JAX's collectives and lax.ppermute only.
A program may use at most 128 MiB of HBM per device.

v0:
```python
import jax
import jax.numpy as jnp
from jax import lax
from jax.sharding import PartitionSpec as P

softcap = 30.0


def local(hidden, head, verdict_ids, row_weight):
    group_rows = hidden.shape[0]
    width = head.shape[1]
    group = lax.axis_index("dp")
    shard = group * lax.axis_size("vocab") + lax.axis_index("vocab")
    gathered = lax.all_gather(hidden, "dp", axis=0, tiled=True)
    raw = jnp.dot(gathered, head, preferred_element_type=jnp.float32)
    capped = softcap * jnp.tanh(raw / softcap)
    expo = jnp.exp(capped - softcap)
    column = shard * width + jnp.arange(width, dtype=jnp.int32)
    onehot = verdict_ids[:, None] == column[None, :]
    partial_total = jnp.sum(expo, axis=1)
    partial_target = jnp.sum(jnp.where(onehot, capped, jnp.float32(0.0)), axis=1)
    total, target = lax.psum((partial_total, partial_target), ("dp", "vocab"))
    log_total = jnp.log(total)
    logprob_all = target - softcap - log_total
    prob = expo * jnp.exp(-log_total)[:, None]
    slope = 1.0 - (capped / softcap) ** 2
    dlog = (row_weight[:, None] * (prob - onehot.astype(jnp.float32)) * slope).astype(jnp.bfloat16)
    head_grad = lax.dot_general(
        gathered, dlog, (((0,), (0,)), ((), ())), preferred_element_type=jnp.float32
    ).astype(jnp.bfloat16)
    logprob = lax.dynamic_slice_in_dim(logprob_all, group * group_rows, group_rows, 0)
    summed = lax.psum_scatter(
        lax.dot_general(
            dlog, head, (((1,), (1,)), ((), ())), preferred_element_type=jnp.float32
        ).astype(jnp.bfloat16),
        "dp",
        scatter_dimension=0,
        tiled=True,
    )
    hidden_grad = lax.psum_scatter(summed, "vocab", scatter_dimension=1, tiled=True).astype(
        jnp.float32
    )
    return (logprob, head_grad, hidden_grad.astype(jnp.bfloat16))


def solution(mesh):
    in_specs = (P("dp", None), P(None, ("dp", "vocab")), P(), P())
    out_specs = (P("dp"), P(None, ("dp", "vocab")), P("dp", "vocab"))
    return jax.shard_map(local, mesh=mesh, in_specs=in_specs, out_specs=out_specs, check_vma=False)
```

profile of v0, /device:TPU:0, one launch (start us, length us, event | category | flops | bytes accessed | tf_op | source)
XLA Modules:
  0.0 285.2 jit_solution(7537608799681178112)
XLA Ops:
  7.2 0.0 all-gather.2.cloned.1.call-start
  7.2 0.7 all-gather.2.cloned.1.call-update
  7.9 0.0 reduce-scatter.5.cloned.1.call-start
  8.0 0.0 copy-start
  8.0 0.0 copy-start.1
  8.0 62.9 %all-gather.2.cloned.1.call-done = bf16[512,4608]{1,0:T(8,128)(2,1)} async-done(((bf16[32,4608]{1,0:T(8,128)(2,1)}), bf16[512,4608]{1,0:T(8,128)(2,1)}) %all-gather.2.cloned.1.call-update) | async-done | bytes 4718608 | tf_op jit(solution)/shard_map/all_gather | solution.py:14
  70.9 9.6 %fusion.6 = (f32[512]{0:T(512)S(1)}, f32[512]{0:T(512)S(1)}, f32[512,1024]{1,0:T(8,128)S(1)}) fusion(s32[1024]{0:T(1024)S(1)} %iota_add_fusion, s32[512]{0:T(512)} %param.6, bf16[512,4608]{1,0:T(8,128)(2,1)} %all-gather.2.cloned.1.call-done, bf16[4608,1024]{1,0:T(8,128)(2,1)} %param.5), kind=kOutput, calls=%fused_computation.12 | convolution fusion | flops 4835507200 | bytes 16263168 | tf_op jit(solution)/shard_map/dot_general | solution.py:15
  80.5 64.6 %all-reduce = (f32[512]{0:T(512)S(1)}, f32[512]{0:T(512)S(1)}) all-reduce(f32[512]{0:T(512)S(1)} %get-tuple-element.10, f32[512]{0:T(512)S(1)} %get-tuple-element.9), channel_id=1, replica_groups=mesh['dp'=16,'vocab'=8] {'dp','vocab'}, use_global_device_ids=true, to_apply=%region_1.2 | all-reduce | flops 1024 | bytes 8192 | tf_op jit(solution)/shard_map/psum | solution.py:22
  145.2 0.0 copy-done
  145.2 0.0 copy-done.1
  145.2 11.0 %convolution_convert_fusion.1 = bf16[512,4608]{1,0:T(8,128)(2,1)} fusion(bf16[4608,1024]{1,0:T(8,128)(2,1)} %param.5, f32[512,1024]{1,0:T(8,128)S(1)} %get-tuple-element.15, f32[512]{0:T(512)S(1)} %get-tuple-element.13, f32[512]{0:T(512)S(1)} %copy-done.1, s32[1024]{0:T(1024)S(1)} %iota_add_fusion, s32[512]{0:T(512)S(1)} %copy-done), kind=kOutput, calls=%fused_computation.2 | convolution fusion | flops 4839964672 | bytes 16263168 | tf_op jit(solution)/shard_map/dot_general | solution.py:33
  156.2 0.0 reduce-scatter.5.cloned.1.call-update
  156.2 0.0 reduce-scatter.7.cloned.1.call-start
  156.2 80.1 %reduce-scatter.5.cloned.1.call-done = bf16[32,4608]{1,0:T(8,128)(2,1)} async-done(((bf16[512,4608]{1,0:T(8,128)(2,1)}), bf16[32,4608]{1,0:T(8,128)(2,1)}) %reduce-scatter.5.cloned.1.call-update) | async-done | bytes 294928 | tf_op jit(solution)/shard_map/reduce_scatter | solution.py:32
  236.3 2.4 copy.9
  238.7 0.0 reduce-scatter.7.cloned.1.call-update
  238.7 10.4 %fusion = bf16[4608,1024]{0,1:T(8,128)(2,1)} fusion(bf16[512,4608]{1,0:T(8,128)(2,1)} %all-gather.2.cloned.1.call-done, f32[512,1024]{1,0:T(8,128)S(1)} %get-tuple-element.15, f32[512]{0:T(512)S(1)} %get-tuple-element.13, f32[512]{0:T(512)S(1)} %copy-done.1, s32[1024]{0:T(1024)S(1)} %iota_add_fusion, s32[512]{0:T(512)S(1)} %copy-done), kind=kOutput, calls=%fused_computation.1 | convolution fusion | flops 4842323968 | bytes 16263168 | tf_op jit(solution)/shard_map/dot_general | solution.py:28
  249.1 12.6 %copy.8 = bf16[4608,1024]{1,0:T(8,128)(2,1)} copy(bf16[4608,1024]{0,1:T(8,128)(2,1)} %fusion) | data formatting | bytes 18874368
  261.7 0.6 dynamic_slice.3
  262.3 14.7 %reduce-scatter.7.cloned.1.call-done = bf16[576,32]{1,0:T(8,128)(2,1)} async-done(((bf16[4608,32]{1,0:T(8,128)(2,1)}), bf16[576,32]{1,0:T(8,128)(2,1)}) %reduce-scatter.7.cloned.1.call-update) | async-done | bytes 36880
  277.0 1.6 copy.10
  (2 shorter events, 0.0 us)
Async XLA Ops:
  7.2 63.7 %all-gather.2.cloned.1.call-start = ((), (), s32[]{:S(2)}) async-start(), calls=%async_computation.2 | async-start | bytes 5013504 | tf_op jit(solution)/shard_map/all_gather | solution.py:14
  7.9 228.4 %reduce-scatter.5.cloned.1.call-start = ((), (), s32[]{:S(2)}) async-start(), calls=%async_computation.3 | async-start | bytes 5013504 | tf_op jit(solution)/shard_map/reduce_scatter | solution.py:32
  8.0 137.2 %copy-start = (s32[512]{0:T(512)S(1)}, s32[512]{0:T(512)}, u32[]{:S(2)}) copy-start(s32[512]{0:T(512)} %param.6) | copy-start | bytes 6148
  8.0 137.2 %copy-start.1 = (f32[512]{0:T(512)S(1)}, f32[512]{0:T(512)}, u32[]{:S(2)}) copy-start(f32[512]{0:T(512)} %param.7) | copy-start | bytes 6148
  156.2 120.8 %reduce-scatter.7.cloned.1.call-start = ((), (), s32[]{:S(2)}) async-start(), calls=%async_computation.4 | async-start | bytes 1327104
Sparse Core Ops, SparseCore 0:
  10.4 60.4 all-gather.1
  156.3 79.9 reduce-scatter.4
  238.8 38.1 reduce-scatter.6
where the time goes:
time: 286 us; the launch traced here: 285 us
  waiting for transfers between devices  158 us (55%)
  blocking collectives  64.6 us (23%)
  matrix products  31 us (11%)
  local copies, waits for them, and re-layouts  17.2 us (6%)
  between operations  13.8 us (5%)
    reduce_scatter x1, waiting for transfers between devices, local(): lax.psum_scatter(lax.dot_general(dlog, head, (((1,), (1,)), ((), ())), pr...  80.1 us
    psum x1, blocking collectives, local(): total, target = lax.psum((partial_total, partial_target), ('dp', 'vocab'))  64.6 us
    all_gather x1, waiting for transfers between devices, local(): gathered = lax.all_gather(hidden, 'dp', axis=0, tiled=True)  62.9 us
    unnamed x7, local copies, waits for them, and re-layouts  16.6 us
    unnamed x4, waiting for transfers between devices  15.5 us
    dot_general x1, matrix products, local(): lax.dot_general(dlog, head, (((1,), (1,)), ((), ())), preferred_element_t...  11 us
    dot_general x1, matrix products, local(): lax.dot_general(gathered, dlog, (((0,), (0,)), ((), ())), preferred_eleme...  10.4 us
    dot_general x1, matrix products, local(): raw = jnp.dot(gathered, head, preferred_element_type=jnp.float32)  9.63 us
  transfers between devices with their start and end apart: 3, of which 3 were waited for; matrix products, arithmetic and copies ran while one was open for 8% of the time, Pallas kernels for 0%

commit v1 on v0

v1 whole, which is shorter than its diff:
```python
import jax
import jax.numpy as jnp
from jax import lax
from jax.sharding import PartitionSpec as P

softcap = 30.0
AXES = ("dp", "vocab")
bf16 = jnp.bfloat16
f32 = jnp.float32


def flips(core0, core1):
    return [(i, i ^ (core1 if i & 8 else core0)) for i in range(128)]


CORE = flips(8, 8)
X1, X2 = flips(16, 48), flips(48, 16)
Y1, Y2 = flips(1, 3), flips(3, 1)
Z1, Z2 = flips(4, 68), flips(68, 4)
ZH = flips(68, 68)


def send(array, partner):
    return lax.ppermute(array, AXES, partner)


def local(hidden, head, verdict_ids, row_weight):
    width = head.shape[1]
    dp = lax.axis_index("dp")
    vocab = lax.axis_index("vocab")
    core, x, zh = dp & 1, (dp >> 1) & 3, dp >> 3
    zl, y = vocab >> 2, vocab & 3
    zero = jnp.zeros_like(core)
    near = 1 + 2 * core
    far = 3 - 2 * core
    mine = jnp.stack([zero, near, far, zero + 2])
    mate = jnp.stack([zero, far, near, zero + 2])

    def ring(own):
        a1, a2 = send(own, X1), send(own, X2)
        return [own, a1, a2, send(a1, X2)]

    own_half = ring(hidden)
    other_half = ring(send(hidden, ZH))
    halves = [
        jnp.concatenate(half + [send(piece, CORE) for piece in half], axis=0)
        for half in (own_half, other_half)
    ]
    blocks = jnp.concatenate(
        [
            ((zh ^ zr) << 3) | ((x ^ slots) << 1) | c
            for zr in (0, 1)
            for slots, c in ((mine, core), (mate, 1 - core))
        ]
    )
    place = blocks[:, None] == jnp.arange(16, dtype=blocks.dtype)[None, :]

    def to_local(whole):
        return jnp.sum(
            jnp.where(place[:, :, None], whole.reshape(1, 16, 32), jnp.zeros((), whole.dtype)), axis=1
        ).reshape(512)

    def to_whole(part):
        return jnp.sum(jnp.where(place[:, :, None], part.reshape(16, 1, 32), 0.0), axis=0)

    ids = to_local(verdict_ids)
    weight = to_local(row_weight)
    column = (dp * 8 + vocab) * width + jnp.arange(width, dtype=jnp.int32)
    onehot = ids[:, None] == column[None, :]

    capped = []
    for half in halves:
        raw = jnp.dot(half, head, preferred_element_type=f32)
        capped.append(softcap * jnp.tanh(raw / softcap))
    capped = jnp.concatenate(capped, axis=0)
    expo = jnp.exp(capped - softcap)
    partial_total = to_whole(jnp.sum(expo, axis=1))
    partial_target = to_whole(jnp.sum(jnp.where(onehot, capped, 0.0), axis=1))
    parcel = jnp.concatenate(
        [
            jnp.broadcast_to(partial_total.reshape(1, 512), (128, 512)),
            jnp.repeat(partial_target, 8, axis=0),
            jnp.zeros((128, 96), f32),
        ],
        axis=1,
    )
    arrived = lax.all_to_all(parcel.reshape(128, 1, 640), AXES, 0, 0, tiled=True)
    sums = jnp.sum(arrived, axis=(0, 1))
    log_total = jnp.log(sums[:512])
    target = sums[512:544]
    own_log = lax.dynamic_slice_in_dim(log_total, dp * 32, 32, 0)
    logprob = target - softcap - own_log
    log_local = to_local(log_total)
    prob = expo * jnp.exp(-log_local)[:, None]
    slope = 1.0 - (capped / softcap) ** 2
    dlog = (weight[:, None] * (prob - onehot.astype(f32)) * slope).astype(bf16)

    def feature_order(slots):
        return jnp.concatenate([((zl ^ zr) << 2) | (y ^ slots) for zr in (0, 1)])

    head_blocks = head.reshape(8, 576, width)

    def terms(rows, slots):
        ordered = head_blocks[feature_order(slots)].reshape(4608, width)
        return lax.dot_general(rows, ordered, (((1,), (1,)), ((), ())), preferred_element_type=f32)

    by_core = dlog.reshape(2, 2, 128, width)
    for_mate = terms(by_core[:, 1].reshape(256, width), mate).astype(bf16)
    for_me = terms(by_core[:, 0].reshape(256, width), mine).astype(bf16)
    got = send(for_mate, CORE)

    def add(a, b):
        return (a.astype(f32) + b.astype(f32)).astype(bf16)

    summed = add(for_me, got).reshape(2, 4, 32, 2, 2304)
    even = core == 0
    z_slots = jnp.stack(
        [
            summed[0, :, :, 0],
            jnp.where(even, summed[0, :, :, 1], summed[1, :, :, 1]),
            jnp.where(even, summed[1, :, :, 1], summed[0, :, :, 1]),
            summed[1, :, :, 0],
        ]
    )
    p = z_slots[:, :, :16]
    q = z_slots[:, :, 16:]
    p = add(p[:, :2], send(p[:, 2:], X2))
    q = add(q[:2], send(q[2:], Z2))
    p = add(p[:, 0], send(p[:, 1], X1))
    q = add(q[0], send(q[1], Z1))
    p = add(p[:2], send(p[2:], Z2))
    q = add(q[:2], send(q[2:], X2))
    p = add(p[0], send(p[1], Z1))
    q = add(q[0], send(q[1], X1))
    pq = jnp.concatenate([p, q], axis=0)
    pq = add(pq[:, :1152], send(pq[:, 1152:], Y2))
    hidden_grad = add(pq[:, :576], send(pq[:, 576:], Y1))

    gathered = jnp.concatenate(halves, axis=0)
    head_grad = lax.dot_general(
        gathered, dlog, (((0,), (0,)), ((), ())), preferred_element_type=f32
    ).astype(bf16)
    return (logprob, head_grad, hidden_grad)


def solution(mesh):
    in_specs = (P("dp", None), P(None, ("dp", "vocab")), P(), P())
    out_specs = (P("dp"), P(None, ("dp", "vocab")), P("dp", "vocab"))
    return jax.shard_map(local, mesh=mesh, in_specs=in_specs, out_specs=out_specs, check_vma=False)
```

time: 286 us -> 164 us (0.57)
  waiting for transfers between devices: 158 us -> 30.9 us
  blocking collectives: 64.6 us -> 0 us
  starting transfers between devices: 0.12 us -> 37.5 us
  local copies, waits for them, and re-layouts: 17.2 us -> 42.5 us
  between operations: 13.8 us -> 0.95 us
  matrix products: 31 us -> 42.3 us
  other arithmetic: 0.01 us -> 9.2 us
    reduce_scatter x1 -> x0, waiting for transfers between devices: 80.1 us -> none  [local(): lax.psum_scatter(lax.dot_general(dlog, head, (((1,), (1,)), ((), ())), pr...]
    psum x1 -> x0, blocking collectives: 64.6 us -> none  [local(): total, target = lax.psum((partial_total, partial_target), ('dp', 'vocab'))]
    all_gather x1 -> x0, waiting for transfers between devices: 62.9 us -> none  [local(): gathered = lax.all_gather(hidden, 'dp', axis=0, tiled=True)]
    ppermute x0 -> x26, waiting for transfers between devices: none -> 28.9 us  [send(): return lax.ppermute(array, AXES, partner)]
    ppermute x0 -> x26, starting transfers between devices: none -> 27.5 us  [send(): return lax.ppermute(array, AXES, partner)]
    gather x0 -> x2, local copies, waits for them, and re-layouts: none -> 18 us  [terms(): ordered = head_blocks[feature_order(slots)].reshape(4608, width)]
    unnamed x4 -> x0, waiting for transfers between devices: 15.5 us -> none
    dot_general x2 -> x4, matrix products: 20.6 us -> 32.1 us  [the longest x2 22.9 us: terms(): lax.dot_general(rows, ordered, (((1,), (1,)), ((), ())), preferred_elemen...]
  transfers between devices with their start and end apart: 3 -> 27, of which waited for: 3 -> 12; matrix products, arithmetic and copies ran while one was open for 8% -> 32% of each run, Pallas kernels for 0% -> 0%
where the time goes in v1:
time: 164 us; the launch traced here: 163 us
  local copies, waits for them, and re-layouts  42.5 us (26%)
  matrix products  42.3 us (26%)
  starting transfers between devices  37.5 us (23%)
  waiting for transfers between devices  30.9 us (19%)
  other arithmetic  9.2 us (6%)
    ppermute x26, waiting for transfers between devices, send(): return lax.ppermute(array, AXES, partner)  28.9 us
    ppermute x26, starting transfers between devices, send(): return lax.ppermute(array, AXES, partner)  27.5 us
    dot_general x2, matrix products, terms(): lax.dot_general(rows, ordered, (((1,), (1,)), ((), ())), preferred_elemen...  22.9 us
    gather x2, local copies, waits for them, and re-layouts, terms(): ordered = head_blocks[feature_order(slots)].reshape(4608, width)  18 us
    unnamed x27, local copies, waits for them, and re-layouts  13.2 us
    dot_general x1, matrix products, local(): lax.dot_general(gathered, dlog, (((0,), (0,)), ((), ())), preferred_eleme...  10.2 us
    all_to_all x1, starting transfers between devices, local(): lax.all_to_all(parcel.reshape(128, 1, 640), AXES, 0, 0, tiled=True)  9.99 us
    dot_general x2, matrix products, local(): raw = jnp.dot(half, head, preferred_element_type=f32)  9.16 us
  transfers between devices with their start and end apart: 27, of which 12 were waited for; matrix products, arithmetic and copies ran while one was open for 32% of the time, Pallas kernels for 0%

profile of v1, /device:TPU:0, one launch (start us, length us, event | category | flops | bytes accessed | tf_op | source)
XLA Modules:
  0.0 163.4 jit_solution(13147158419032973839)
XLA Ops:
  0.6 1.7 %collective-permute-start = (bf16[32,4608]{1,0:T(8,128)(2,1)}, bf16[32,4608]{1,0:T(8,128)(2,1)S(1)}, u32[]{:S(2)}, u32[]{:S(2)}) collective-permute-start(bf16[32,4608]{1,0:T(8,128)(2,1)} %param.4), channel_id=1, source_target_pairs={{0,16},{1,17},{2,18},{3,19},{4,20},{5,21},{6,22},{7,23},{8,56},{9,... | collective-permute-start | bytes 884744 | tf_op jit(solution)/shard_map/ppermute | solution.py:24
  2.3 2.1 %collective-permute-start.1 = (bf16[32,4608]{1,0:T(8,128)(2,1)}, bf16[32,4608]{1,0:T(8,128)(2,1)S(1)}, u32[]{:S(2)}, u32[]{:S(2)}) collective-permute-start(bf16[32,4608]{1,0:T(8,128)(2,1)} %param.4), channel_id=1, source_target_pairs={{0,48},{1,49},{2,50},{3,51},{4,52},{5,53},{6,54},{7,55},{8,24},{9,... | collective-permute-start | bytes 884744 | tf_op jit(solution)/shard_map/ppermute | solution.py:24
  4.4 4.0 %collective-permute-start.7 = (bf16[32,4608]{1,0:T(8,128)(2,1)}, bf16[32,4608]{1,0:T(8,128)(2,1)S(1)}, u32[]{:S(2)}, u32[]{:S(2)}) collective-permute-start(bf16[32,4608]{1,0:T(8,128)(2,1)} %param.4), channel_id=1, source_target_pairs={{0,68},{1,69},{2,70},{3,71},{4,64},{5,65},{6,66},{7,67},{8,76},{9,... | collective-permute-start | bytes 884744 | tf_op jit(solution)/shard_map/ppermute | solution.py:24
  8.4 1.8 %constant_dynamic-update-slice_fusion.31 = (bf16[512,4608]{1,0:T(8,128)(2,1)}, bf16[256,4608]{1,0:T(8,128)(2,1)}) fusion(bf16[32,4608]{1,0:T(8,128)(2,1)} %param.4), kind=kLoop, calls=%fused_computation.100 | loop fusion | bytes 884736
  12.4 1.2 collective-permute-start.2
  14.1 2.2 %collective-permute-done.7 = bf16[32,4608]{1,0:T(8,128)(2,1)S(1)} collective-permute-done((bf16[32,4608]{1,0:T(8,128)(2,1)}, bf16[32,4608]{1,0:T(8,128)(2,1)S(1)}, u32[]{:S(2)}, u32[]{:S(2)}) %collective-permute-start.7) | collective-permute-done | bytes 294944 | tf_op jit(solution)/shard_map/ppermute | solution.py:24
  18.6 2.0 %collective-permute-done.2 = bf16[32,4608]{1,0:T(8,128)(2,1)S(1)} collective-permute-done((bf16[32,4608]{1,0:T(8,128)(2,1)S(1)}, bf16[32,4608]{1,0:T(8,128)(2,1)S(1)}, u32[]{:S(2)}, u32[]{:S(2)}) %collective-permute-start.2) | collective-permute-done | bytes 294944 | tf_op jit(solution)/shard_map/ppermute | solution.py:24
  24.6 1.5 collective-permute-start.10
  26.9 1.6 collective-permute-done.9
  30.3 6.5 %fusion.7 = f32[256,1024]{1,0:T(8,128)S(1)} fusion(bf16[256,4608]{1,0:T(8,128)(2,1)} %get-tuple-element.39, bf16[4608,1024]{1,0:T(8,128)(2,1)} %param.5), kind=kOutput, calls=%fused_computation.21 | convolution fusion | flops 2416443392 | bytes 12845056 | tf_op jit(solution)/shard_map/dot_general | solution.py:73
  43.4 2.6 %fusion.9 = f32[256,1024]{1,0:T(8,128)S(1)} fusion(bf16[256,4608]{1,0:T(8,128)(2,1)S(1)} %get-tuple-element.23, bf16[4608,1024]{1,0:T(8,128)(2,1)S(1)} %bitcast.75), kind=kOutput, calls=%fused_computation.23 | convolution fusion | flops 2416443392 | bytes 12845056 | tf_op jit(solution)/shard_map/dot_general | solution.py:73
  46.1 2.1 %fusion.24 = (f32[512]{0:T(512)S(1)}, f32[512]{0:T(512)S(1)}, f32[512,1024]{1,0:T(8,128)S(1)}, f32[512,1024]{1,0:T(8,128)}) fusion(f32[256,1024]{1,0:T(8,128)S(1)} %fusion.9, f32[256,1024]{1,0:T(8,128)S(1)} %fusion.7, s32[1024]{0:T(1024)S(1)} %iota_add_fusion, s32[512]{0:T(512)S(1)} %eq.47), kind=kLoop, calls=%fused_computation.130 | loop fusion | flops 4717568 | bytes 6301696 | tf_op jit(solution)/shard_map/reduce_sum | solution.py:77
  49.5 10.0 %all-to-all-start = ((f32[128,1,640]{2,1,0:T(1,128)}), f32[128,1,640]{2,1,0:T(1,128)S(1)}, u32[]{:S(2)}, u32[]{:S(2)}) async-start(f32[128,1,640]{2,1,0:T(1,128)} %reshape.617), calls=%async_computation | async-start | bytes 655360 | tf_op jit(solution)/shard_map/all_to_all | solution.py:87
  59.7 9.0 %gather_fusion.1 = bf16[8,576,1024]{2,1,0:T(8,128)(2,1)} fusion(bf16[8,576,1024]{2,1,0:T(8,128)(2,1)} %bitcast.72, s32[1024]{0:T(1024)S(1)} %pad_clamp_fusion), kind=kCustom, calls=%fused_computation.1 | custom fusion | bytes 18874400 | tf_op jit(solution)/shard_map/gather | solution.py:104
  68.7 2.0 %all-to-all-done = f32[128,1,640]{2,1,0:T(1,128)S(1)} async-done(((f32[128,1,640]{2,1,0:T(1,128)}), f32[128,1,640]{2,1,0:T(1,128)S(1)}, u32[]{:S(2)}, u32[]{:S(2)}) %all-to-all-start) | async-done | bytes 327712 | tf_op jit(solution)/shard_map/all_to_all | solution.py:87
  71.3 2.1 %multiply_convert_fusion = bf16[2,2,128,1024]{3,2,1,0:T(8,128)(2,1)S(1)} fusion(f32[2,2,128,1024]{3,2,1,0:T(8,128)} %bitcast.85, f32[2,2,128,1024]{3,2,1,0:T(8,128)S(1)} %bitcast.84, s32[1024]{0:T(1024)S(1)} %iota_add_fusion, s32[2,2,128]{2,1,0:T(2,128)S(1)} %eq.51, f32[2,2,128]{2,1,0:T(2,128)S(1)} %exp.25, f32[2,2,128]{2,1,0:T(2,128)S(1)} %mul.67), kind=kLoop, calls=%fused_computation.15 | loop fusion | flops 3670016 | bytes 5253120 | tf_op jit(solution)/shard_map/convert_element_type | solution.py:96
  73.5 11.3 %convolution_convert_fusion.1 = bf16[256,4608]{1,0:T(8,128)(2,1)} fusion(bf16[256,1024]{1,0:T(8,128)(2,1)S(1)} %bitcast.87, bf16[4608,1024]{1,0:T(8,128)(2,1)} %bitcast.82), kind=kOutput, calls=%fused_computation.3 | convolution fusion | flops 2417098752 | bytes 12320768 | tf_op jit(solution)/shard_map/dot_general | solution.py:105
  84.8 9.0 %gather_fusion = bf16[8,576,1024]{2,1,0:T(8,128)(2,1)} fusion(bf16[8,576,1024]{2,1,0:T(8,128)(2,1)} %bitcast.73, s32[1024]{0:T(1024)S(1)} %pad_clamp_fusion.1), kind=kCustom, calls=%fused_computation | custom fusion | bytes 18874400 | tf_op jit(solution)/shard_map/gather | solution.py:104
  93.8 11.7 %add_convert_fusion = bf16[256,4608]{1,0:T(8,128)(2,1)} fusion(bf16[256,4608]{1,0:T(8,128)(2,1)} %collective-permute-done.15, bf16[256,1024]{1,0:T(8,128)(2,1)S(1)} %bitcast.86, bf16[4608,1024]{1,0:T(8,128)(2,1)} %bitcast.83), kind=kOutput, calls=%fused_computation.6 | convolution fusion | flops 2421817344 | bytes 14680064 | tf_op jit(solution)/shard_map/dot_general | solution.py:105
  105.5 2.6 %reshape.621 = bf16[2,4,32,2,2304]{4,3,2,1,0:T(2,128)(2,1)S(1)} reshape(bf16[256,4608]{1,0:T(8,128)(2,1)} %add_convert_fusion) | data formatting | bytes 4718592 | tf_op jit(solution)/shard_map/reshape | solution.py:115
  108.1 4.4 %fusion.25 = (bf16[1,4,32,1,2304]{4,3,2,1,0:T(2,128)(2,1)S(1)}, bf16[1,4,32,1,2304]{4,3,2,1,0:T(2,128)(2,1)S(1)}, bf16[1,4,32,1,2304]{4,3,2,1,0:T(2,128)(2,1)S(1)}, bf16[1,4,32,1,2304]{4,3,2,1,0:T(2,128)(2,1)S(1)}) fusion(bf16[2,4,32,2,2304]{4,3,2,1,0:T(2,128)(2,1)S(1)} %reshape.621), kind=kLoop, calls=%fused_computation.131 | loop fusion | bytes 4718592 | tf_op jit(solution)/shard_map/slice | solution.py:119
  114.8 2.7 %collective-permute-start.20 = (bf16[2,4,16,2304]{3,2,1,0:T(8,128)(2,1)S(1)}, bf16[2,4,16,2304]{3,2,1,0:T(8,128)(2,1)S(1)}, u32[]{:S(2)}, u32[]{:S(2)}) collective-permute-start(bf16[2,4,16,2304]{3,2,1,0:T(8,128)(2,1)S(1)} %pad_maximum_fusion.1), channel_id=1, source_target_pairs={{0,68},{1,69},{2,70},{3,71},{4,64},{5,65},{6,66},{7,67},{8,12},{9,... | collective-permute-start | bytes 1769480 | tf_op jit(solution)/shard_map/ppermute | solution.py:24
  117.5 7.6 %collective-permute-done.16 = bf16[4,2,16,2304]{3,2,1,0:T(8,128)(2,1)} collective-permute-done((bf16[4,2,16,2304]{3,2,1,0:T(8,128)(2,1)}, bf16[4,2,16,2304]{3,2,1,0:T(8,128)(2,1)}, u32[]{:S(2)}, u32[]{:S(2)}) %collective-permute-start.16) | collective-permute-done | bytes 589856 | tf_op jit(solution)/shard_map/ppermute | solution.py:24
  125.1 1.2 add_convert_fusion.2
  127.5 5.6 %collective-permute-done.17 = bf16[4,16,2304]{2,1,0:T(8,128)(2,1)S(1)} collective-permute-done((bf16[4,16,2304]{2,1,0:T(8,128)(2,1)S(1)}, bf16[4,16,2304]{2,1,0:T(8,128)(2,1)S(1)}, u32[]{:S(2)}, u32[]{:S(2)}) %collective-permute-start.17) | collective-permute-done | bytes 294944 | tf_op jit(solution)/shard_map/ppermute | solution.py:24
  134.3 2.7 %collective-permute-start.22 = (bf16[2,16,2304]{2,1,0:T(8,128)(2,1)S(1)}, bf16[2,16,2304]{2,1,0:T(8,128)(2,1)S(1)}, u32[]{:S(2)}, u32[]{:S(2)}) collective-permute-start(bf16[2,16,2304]{2,1,0:T(8,128)(2,1)S(1)} %slice.147), channel_id=1, source_target_pairs={{0,48},{1,49},{2,50},{3,51},{4,52},{5,53},{6,54},{7,55},{8,24},{9,... | collective-permute-start | bytes 442376 | tf_op jit(solution)/shard_map/ppermute | solution.py:24
  137.0 2.6 %collective-permute-done.18 = bf16[2,16,2304]{2,1,0:T(8,128)(2,1)S(1)} collective-permute-done((bf16[2,16,2304]{2,1,0:T(8,128)(2,1)S(1)}, bf16[2,16,2304]{2,1,0:T(8,128)(2,1)S(1)}, u32[]{:S(2)}, u32[]{:S(2)}) %collective-permute-start.18) | collective-permute-done | bytes 147488 | tf_op jit(solution)/shard_map/ppermute | solution.py:24
  140.8 2.1 %collective-permute-start.23 = (bf16[16,2304]{1,0:T(8,128)(2,1)S(1)}, bf16[16,2304]{1,0:T(8,128)(2,1)S(1)}, u32[]{:S(2)}, u32[]{:S(2)}) collective-permute-start(bf16[16,2304]{1,0:T(8,128)(2,1)S(1)} %slice_bitcast_fusion.4), channel_id=1, source_target_pairs={{0,16},{1,17},{2,18},{3,19},{4,20},{5,21},{6,22},{7,23},{8,56},{9,... | collective-permute-start | bytes 221192 | tf_op jit(solution)/shard_map/ppermute | solution.py:24
  142.9 1.2 collective-permute-done.19
  145.3 3.0 %collective-permute-start.24 = (bf16[32,1152]{1,0:T(8,128)(2,1)S(1)}, bf16[32,1152]{1,0:T(8,128)(2,1)S(1)}, u32[]{:S(2)}, u32[]{:S(2)}) collective-permute-start(bf16[32,1152]{1,0:T(8,128)(2,1)S(1)} %pad_maximum_fusion.6), channel_id=1, source_target_pairs={{0,3},{1,2},{2,1},{3,0},{4,7},{5,6},{6,5},{7,4},{8,9},{9,8},{10,11... | collective-permute-start | bytes 221192 | tf_op jit(solution)/shard_map/ppermute | solution.py:24
  148.3 10.2 %convolution_convert_fusion = bf16[4608,1024]{1,0:T(8,128)(2,1)} fusion(bf16[512,4608]{1,0:T(8,128)(2,1)} %get-tuple-element.22, f32[512]{0:T(512)S(1)} %exp.23, f32[512]{0:T(512)S(1)} %mul.61, s32[1024]{0:T(1024)S(1)} %iota_add_fusion, s32[512]{0:T(512)S(1)} %eq.47, f32[256,1024]{1,0:T(8,128)S(1)} %copy-done.1, f32[256,1024]{1,0:T(8,128)S(1)} %fusion.7), kind=kOutput, calls=%fused_computation.2 | convolution fusion | flops 4842848256 | bytes 16263168 | tf_op jit(solution)/shard_map/dot_general | solution.py:140
  159.5 3.2 %collective-permute-done.25 = bf16[32,576]{1,0:T(8,128)(2,1)S(1)} collective-permute-done((bf16[32,576]{1,0:T(8,128)(2,1)S(1)}, bf16[32,576]{1,0:T(8,128)(2,1)S(1)}, u32[]{:S(2)}, u32[]{:S(2)}) %collective-permute-start.25) | collective-permute-done | bytes 36896 | tf_op jit(solution)/shard_map/ppermute | solution.py:24
  (119 shorter events, 28.9 us)
Async XLA Ops:
  0.6 11.8 %collective-permute-start = (bf16[32,4608]{1,0:T(8,128)(2,1)}, bf16[32,4608]{1,0:T(8,128)(2,1)S(1)}, u32[]{:S(2)}, u32[]{:S(2)}) collective-permute-start(bf16[32,4608]{1,0:T(8,128)(2,1)} %param.4), channel_id=1, source_target_pairs={{0,16},{1,17},{2,18},{3,19},{4,20},{5,21},{6,22},{7,23},{8,56},{9,... | collective-permute-start | bytes 884744 | tf_op jit(solution)/shard_map/ppermute | solution.py:24
  2.3 11.3 %collective-permute-start.1 = (bf16[32,4608]{1,0:T(8,128)(2,1)}, bf16[32,4608]{1,0:T(8,128)(2,1)S(1)}, u32[]{:S(2)}, u32[]{:S(2)}) collective-permute-start(bf16[32,4608]{1,0:T(8,128)(2,1)} %param.4), channel_id=1, source_target_pairs={{0,48},{1,49},{2,50},{3,51},{4,52},{5,53},{6,54},{7,55},{8,24},{9,... | collective-permute-start | bytes 884744 | tf_op jit(solution)/shard_map/ppermute | solution.py:24
  4.4 18.2 %collective-permute-start.3 = (bf16[32,4608]{1,0:T(8,128)(2,1)}, bf16[32,4608]{1,0:T(8,128)(2,1)S(1)}, u32[]{:S(2)}, u32[]{:S(2)}) collective-permute-start(bf16[32,4608]{1,0:T(8,128)(2,1)} %param.4), channel_id=1, source_target_pairs={{0,8},{1,9},{2,10},{3,11},{4,12},{5,13},{6,14},{7,15},{8,0},{9,1},... | collective-permute-start | bytes 884744 | tf_op jit(solution)/shard_map/ppermute | solution.py:24
  4.4 11.9 %collective-permute-start.7 = (bf16[32,4608]{1,0:T(8,128)(2,1)}, bf16[32,4608]{1,0:T(8,128)(2,1)S(1)}, u32[]{:S(2)}, u32[]{:S(2)}) collective-permute-start(bf16[32,4608]{1,0:T(8,128)(2,1)} %param.4), channel_id=1, source_target_pairs={{0,68},{1,69},{2,70},{3,71},{4,64},{5,65},{6,66},{7,67},{8,76},{9,... | collective-permute-start | bytes 884744 | tf_op jit(solution)/shard_map/ppermute | solution.py:24
  12.4 8.2 %collective-permute-start.2 = (bf16[32,4608]{1,0:T(8,128)(2,1)S(1)}, bf16[32,4608]{1,0:T(8,128)(2,1)S(1)}, u32[]{:S(2)}, u32[]{:S(2)}) collective-permute-start(bf16[32,4608]{1,0:T(8,128)(2,1)S(1)} %collective-permute-done), channel_id=1, source_target_pairs={{0,48},{1,49},{2,50},{3,51},{4,52},{5,53},{6,54},{7,55},{8,24},{9,... | collective-permute-start | bytes 884744 | tf_op jit(solution)/shard_map/ppermute | solution.py:24
  13.6 9.9 %collective-permute-start.4 = (bf16[32,4608]{1,0:T(8,128)(2,1)S(1)}, bf16[32,4608]{1,0:T(8,128)(2,1)S(1)}, u32[]{:S(2)}, u32[]{:S(2)}) collective-permute-start(bf16[32,4608]{1,0:T(8,128)(2,1)S(1)} %collective-permute-done), channel_id=1, source_target_pairs={{0,8},{1,9},{2,10},{3,11},{4,12},{5,13},{6,14},{7,15},{8,0},{9,1},... | collective-permute-start | bytes 884744 | tf_op jit(solution)/shard_map/ppermute | solution.py:24
  13.6 13.4 %collective-permute-start.5 = (bf16[32,4608]{1,0:T(8,128)(2,1)S(1)}, bf16[32,4608]{1,0:T(8,128)(2,1)S(1)}, u32[]{:S(2)}, u32[]{:S(2)}) collective-permute-start(bf16[32,4608]{1,0:T(8,128)(2,1)S(1)} %collective-permute-done.1), channel_id=1, source_target_pairs={{0,8},{1,9},{2,10},{3,11},{4,12},{5,13},{6,14},{7,15},{8,0},{9,1},... | collective-permute-start | bytes 884744 | tf_op jit(solution)/shard_map/ppermute | solution.py:24
  16.3 8.3 %collective-permute-start.8 = (bf16[32,4608]{1,0:T(8,128)(2,1)S(1)}, bf16[32,4608]{1,0:T(8,128)(2,1)S(1)}, u32[]{:S(2)}, u32[]{:S(2)}) collective-permute-start(bf16[32,4608]{1,0:T(8,128)(2,1)S(1)} %collective-permute-done.7), channel_id=1, source_target_pairs={{0,16},{1,17},{2,18},{3,19},{4,20},{5,21},{6,22},{7,23},{8,56},{9,... | collective-permute-start | bytes 884744 | tf_op jit(solution)/shard_map/ppermute | solution.py:24
  20.6 7.9 %collective-permute-start.9 = (bf16[32,4608]{1,0:T(8,128)(2,1)S(1)}, bf16[32,4608]{1,0:T(8,128)(2,1)S(1)}, u32[]{:S(2)}, u32[]{:S(2)}) collective-permute-start(bf16[32,4608]{1,0:T(8,128)(2,1)S(1)} %collective-permute-done.7), channel_id=1, source_target_pairs={{0,48},{1,49},{2,50},{3,51},{4,52},{5,53},{6,54},{7,55},{8,24},{9,... | collective-permute-start | bytes 884744 | tf_op jit(solution)/shard_map/ppermute | solution.py:24
  22.6 17.8 %collective-permute-start.11 = (bf16[32,4608]{1,0:T(8,128)(2,1)S(1)}, bf16[32,4608]{1,0:T(8,128)(2,1)S(1)}, u32[]{:S(2)}, u32[]{:S(2)}) collective-permute-start(bf16[32,4608]{1,0:T(8,128)(2,1)S(1)} %collective-permute-done.7), channel_id=1, source_target_pairs={{0,8},{1,9},{2,10},{3,11},{4,12},{5,13},{6,14},{7,15},{8,0},{9,1},... | collective-permute-start | bytes 884744 | tf_op jit(solution)/shard_map/ppermute | solution.py:24
  23.5 5.9 %collective-permute-start.6 = (bf16[32,4608]{1,0:T(8,128)(2,1)S(1)}, bf16[32,4608]{1,0:T(8,128)(2,1)S(1)}, u32[]{:S(2)}, u32[]{:S(2)}) collective-permute-start(bf16[32,4608]{1,0:T(8,128)(2,1)S(1)} %collective-permute-done.2), channel_id=1, source_target_pairs={{0,8},{1,9},{2,10},{3,11},{4,12},{5,13},{6,14},{7,15},{8,0},{9,1},... | collective-permute-start | bytes 884744 | tf_op jit(solution)/shard_map/ppermute | solution.py:24
  24.6 13.0 %collective-permute-start.10 = (bf16[32,4608]{1,0:T(8,128)(2,1)S(1)}, bf16[32,4608]{1,0:T(8,128)(2,1)S(1)}, u32[]{:S(2)}, u32[]{:S(2)}) collective-permute-start(bf16[32,4608]{1,0:T(8,128)(2,1)S(1)} %collective-permute-done.8), channel_id=1, source_target_pairs={{0,48},{1,49},{2,50},{3,51},{4,52},{5,53},{6,54},{7,55},{8,24},{9,... | collective-permute-start | bytes 884744 | tf_op jit(solution)/shard_map/ppermute | solution.py:24
  26.9 14.2 %collective-permute-start.12 = (bf16[32,4608]{1,0:T(8,128)(2,1)S(1)}, bf16[32,4608]{1,0:T(8,128)(2,1)S(1)}, u32[]{:S(2)}, u32[]{:S(2)}) collective-permute-start(bf16[32,4608]{1,0:T(8,128)(2,1)S(1)} %collective-permute-done.8), channel_id=1, source_target_pairs={{0,8},{1,9},{2,10},{3,11},{4,12},{5,13},{6,14},{7,15},{8,0},{9,1},... | collective-permute-start | bytes 884744 | tf_op jit(solution)/shard_map/ppermute | solution.py:24
  28.6 13.3 %collective-permute-start.13 = (bf16[32,4608]{1,0:T(8,128)(2,1)S(1)}, bf16[32,4608]{1,0:T(8,128)(2,1)S(1)}, u32[]{:S(2)}, u32[]{:S(2)}) collective-permute-start(bf16[32,4608]{1,0:T(8,128)(2,1)S(1)} %collective-permute-done.9), channel_id=1, source_target_pairs={{0,8},{1,9},{2,10},{3,11},{4,12},{5,13},{6,14},{7,15},{8,0},{9,1},... | collective-permute-start | bytes 884744 | tf_op jit(solution)/shard_map/ppermute | solution.py:24
  29.4 14.0 %slice-start = ((s8[9437184]{0:T(1024)(128)(4,1)}), s8[4194304]{0:T(1024)(128)(4,1)S(1)}, s32[]{:S(2)}) async-start(s8[9437184]{0:T(1024)(128)(4,1)} %bitcast.74), calls=%async_computation.1 | async-start | bytes 8388608
  30.3 13.1 %slice-start.1 = ((s8[9437184]{0:T(1024)(128)(4,1)}), s8[4194304]{0:T(1024)(128)(4,1)S(1)}, s32[]{:S(2)}) async-start(s8[9437184]{0:T(1024)(128)(4,1)} %bitcast.74), calls=%async_computation.2 | async-start | bytes 8388608
  30.3 13.1 %slice-start.2 = ((s8[9437184]{0:T(1024)(128)(4,1)}), s8[1048576]{0:T(1024)(128)(4,1)S(1)}, s32[]{:S(2)}) async-start(s8[9437184]{0:T(1024)(128)(4,1)} %bitcast.74), calls=%async_computation.3 | async-start | bytes 2097152
  37.6 5.0 %collective-permute-start.14 = (bf16[32,4608]{1,0:T(8,128)(2,1)S(1)}, bf16[32,4608]{1,0:T(8,128)(2,1)S(1)}, u32[]{:S(2)}, u32[]{:S(2)}) collective-permute-start(bf16[32,4608]{1,0:T(8,128)(2,1)S(1)} %collective-permute-done.10), channel_id=1, source_target_pairs={{0,8},{1,9},{2,10},{3,11},{4,12},{5,13},{6,14},{7,15},{8,0},{9,1},... | collective-permute-start | bytes 884744 | tf_op jit(solution)/shard_map/ppermute | solution.py:24
  46.1 2.1 %copy-start = (f32[256,1024]{1,0:T(8,128)}, f32[256,1024]{1,0:T(8,128)S(1)}, u32[]{:S(2)}) copy-start(f32[256,1024]{1,0:T(8,128)S(1)} %fusion.9) | copy-start | bytes 3145732
  49.5 21.2 %all-to-all-start = ((f32[128,1,640]{2,1,0:T(1,128)}), f32[128,1,640]{2,1,0:T(1,128)S(1)}, u32[]{:S(2)}, u32[]{:S(2)}) async-start(f32[128,1,640]{2,1,0:T(1,128)} %reshape.617), calls=%async_computation | async-start | bytes 655360 | tf_op jit(solution)/shard_map/all_to_all | solution.py:87
  84.7 9.1 %collective-permute-start.15 = (bf16[256,4608]{1,0:T(8,128)(2,1)}, bf16[256,4608]{1,0:T(8,128)(2,1)}, u32[]{:S(2)}, u32[]{:S(2)}) collective-permute-start(bf16[256,4608]{1,0:T(8,128)(2,1)} %convolution_convert_fusion.1), channel_id=1, source_target_pairs={{0,8},{1,9},{2,10},{3,11},{4,12},{5,13},{6,14},{7,15},{8,0},{9,1},... | collective-permute-start | bytes 7077896 | tf_op jit(solution)/shard_map/ppermute | solution.py:24
  113.7 11.4 %collective-permute-start.16 = (bf16[4,2,16,2304]{3,2,1,0:T(8,128)(2,1)}, bf16[4,2,16,2304]{3,2,1,0:T(8,128)(2,1)}, u32[]{:S(2)}, u32[]{:S(2)}) collective-permute-start(bf16[4,2,16,2304]{3,2,1,0:T(8,128)(2,1)} %pad_maximum_fusion.3), channel_id=1, source_target_pairs={{0,48},{1,49},{2,50},{3,51},{4,52},{5,53},{6,54},{7,55},{8,24},{9,... | collective-permute-start | bytes 1769480 | tf_op jit(solution)/shard_map/ppermute | solution.py:24
  114.8 11.6 %collective-permute-start.20 = (bf16[2,4,16,2304]{3,2,1,0:T(8,128)(2,1)S(1)}, bf16[2,4,16,2304]{3,2,1,0:T(8,128)(2,1)S(1)}, u32[]{:S(2)}, u32[]{:S(2)}) collective-permute-start(bf16[2,4,16,2304]{3,2,1,0:T(8,128)(2,1)S(1)} %pad_maximum_fusion.1), channel_id=1, source_target_pairs={{0,68},{1,69},{2,70},{3,71},{4,64},{5,65},{6,66},{7,67},{8,12},{9,... | collective-permute-start | bytes 1769480 | tf_op jit(solution)/shard_map/ppermute | solution.py:24
  126.3 6.8 %collective-permute-start.17 = (bf16[4,16,2304]{2,1,0:T(8,128)(2,1)S(1)}, bf16[4,16,2304]{2,1,0:T(8,128)(2,1)S(1)}, u32[]{:S(2)}, u32[]{:S(2)}) collective-permute-start(bf16[4,16,2304]{2,1,0:T(8,128)(2,1)S(1)} %slice_bitcast_fusion.2), channel_id=1, source_target_pairs={{0,16},{1,17},{2,18},{3,19},{4,20},{5,21},{6,22},{7,23},{8,56},{9,... | collective-permute-start | bytes 884744 | tf_op jit(solution)/shard_map/ppermute | solution.py:24
  126.5 21.8 %copy-start.1 = (f32[256,1024]{1,0:T(8,128)S(1)}, f32[256,1024]{1,0:T(8,128)}, u32[]{:S(2)}) copy-start(f32[256,1024]{1,0:T(8,128)} %copy-done) | copy-start | bytes 3145732
  126.6 7.6 %collective-permute-start.21 = (bf16[4,16,2304]{2,1,0:T(8,128)(2,1)S(1)}, bf16[4,16,2304]{2,1,0:T(8,128)(2,1)S(1)}, u32[]{:S(2)}, u32[]{:S(2)}) collective-permute-start(bf16[4,16,2304]{2,1,0:T(8,128)(2,1)S(1)} %slice_bitcast_fusion), channel_id=1, source_target_pairs={{0,4},{1,5},{2,6},{3,7},{4,0},{5,1},{6,2},{7,3},{8,76},{9,77},{10,... | collective-permute-start | bytes 884744 | tf_op jit(solution)/shard_map/ppermute | solution.py:24
  133.2 6.4 %collective-permute-start.18 = (bf16[2,16,2304]{2,1,0:T(8,128)(2,1)S(1)}, bf16[2,16,2304]{2,1,0:T(8,128)(2,1)S(1)}, u32[]{:S(2)}, u32[]{:S(2)}) collective-permute-start(bf16[2,16,2304]{2,1,0:T(8,128)(2,1)S(1)} %slice.141), channel_id=1, source_target_pairs={{0,68},{1,69},{2,70},{3,71},{4,64},{5,65},{6,66},{7,67},{8,12},{9,... | collective-permute-start | bytes 442376 | tf_op jit(solution)/shard_map/ppermute | solution.py:24
  134.3 6.4 %collective-permute-start.22 = (bf16[2,16,2304]{2,1,0:T(8,128)(2,1)S(1)}, bf16[2,16,2304]{2,1,0:T(8,128)(2,1)S(1)}, u32[]{:S(2)}, u32[]{:S(2)}) collective-permute-start(bf16[2,16,2304]{2,1,0:T(8,128)(2,1)S(1)} %slice.147), channel_id=1, source_target_pairs={{0,48},{1,49},{2,50},{3,51},{4,52},{5,53},{6,54},{7,55},{8,24},{9,... | collective-permute-start | bytes 442376 | tf_op jit(solution)/shard_map/ppermute | solution.py:24
  139.7 4.4 %collective-permute-start.19 = (bf16[16,2304]{1,0:T(8,128)(2,1)S(1)}, bf16[16,2304]{1,0:T(8,128)(2,1)S(1)}, u32[]{:S(2)}, u32[]{:S(2)}) collective-permute-start(bf16[16,2304]{1,0:T(8,128)(2,1)S(1)} %slice_bitcast_fusion.6), channel_id=1, source_target_pairs={{0,4},{1,5},{2,6},{3,7},{4,0},{5,1},{6,2},{7,3},{8,76},{9,77},{10,... | collective-permute-start | bytes 221192 | tf_op jit(solution)/shard_map/ppermute | solution.py:24
  140.8 4.5 %collective-permute-start.23 = (bf16[16,2304]{1,0:T(8,128)(2,1)S(1)}, bf16[16,2304]{1,0:T(8,128)(2,1)S(1)}, u32[]{:S(2)}, u32[]{:S(2)}) collective-permute-start(bf16[16,2304]{1,0:T(8,128)(2,1)S(1)} %slice_bitcast_fusion.4), channel_id=1, source_target_pairs={{0,16},{1,17},{2,18},{3,19},{4,20},{5,21},{6,22},{7,23},{8,56},{9,... | collective-permute-start | bytes 221192 | tf_op jit(solution)/shard_map/ppermute | solution.py:24
  145.3 13.3 %collective-permute-start.24 = (bf16[32,1152]{1,0:T(8,128)(2,1)S(1)}, bf16[32,1152]{1,0:T(8,128)(2,1)S(1)}, u32[]{:S(2)}, u32[]{:S(2)}) collective-permute-start(bf16[32,1152]{1,0:T(8,128)(2,1)S(1)} %pad_maximum_fusion.6), channel_id=1, source_target_pairs={{0,3},{1,2},{2,1},{3,0},{4,7},{5,6},{6,5},{7,4},{8,9},{9,8},{10,11... | collective-permute-start | bytes 221192 | tf_op jit(solution)/shard_map/ppermute | solution.py:24
  158.6 4.1 %collective-permute-start.25 = (bf16[32,576]{1,0:T(8,128)(2,1)S(1)}, bf16[32,576]{1,0:T(8,128)(2,1)S(1)}, u32[]{:S(2)}, u32[]{:S(2)}) collective-permute-start(bf16[32,576]{1,0:T(8,128)(2,1)S(1)} %slice.153), channel_id=1, source_target_pairs={{0,1},{1,0},{2,3},{3,2},{4,5},{5,4},{6,7},{7,6},{8,11},{9,10},{10,... | collective-permute-start | bytes 110600 | tf_op jit(solution)/shard_map/ppermute | solution.py:24

commit v2 on v1

v2 whole, which is shorter than its diff:
```python
import functools

import jax
import jax.numpy as jnp
from jax import lax
from jax.experimental import pallas as pl
from jax.experimental.pallas import tpu as pltpu
from jax.sharding import PartitionSpec as P

softcap = 30.0
AXES = ("dp", "vocab")
bf16 = jnp.bfloat16
f32 = jnp.float32
D = 4608
WIDTH = 1024
FEATURES = 576


def flips(core0, core1):
    return [(i, i ^ (core1 if i & 8 else core0)) for i in range(128)]


CORE = flips(8, 8)
X1, X2 = flips(16, 48), flips(48, 16)
Y1, Y2 = flips(1, 3), flips(3, 1)
Z1, Z2 = flips(4, 68), flips(68, 4)
ZH = flips(68, 68)


def send(array, partner):
    return lax.ppermute(array, AXES, partner)


def params(mib):
    return pltpu.CompilerParams(vmem_limit_bytes=mib << 20)


def cost(flops, moved):
    return pl.CostEstimate(flops=flops, bytes_accessed=moved, transcendentals=0)


def forward_kernel(base_ref, *refs):
    pieces, (ids_ref, head_ref, capped_ref, total_ref, target_ref, rows, sums, hits) = refs[:8], refs[8:]
    step = pl.program_id(0)

    @pl.when(step == 0)
    def _():
        for i in range(8):
            rows[32 * i : 32 * i + 32, :] = pieces[i][...]
        sums[...] = jnp.zeros_like(sums)
        hits[...] = jnp.zeros_like(hits)

    raw = jnp.dot(rows[...], head_ref[...], preferred_element_type=f32)
    capped = softcap * jnp.tanh(raw / softcap)
    capped_ref[...] = capped
    ids = ids_ref[...]
    lane = lax.broadcasted_iota(jnp.int32, (256, 128), 1)
    total = sums[...]
    hit = hits[...]
    for j in range(2):
        part = capped[:, 128 * j : 128 * j + 128]
        total = total + jnp.exp(part - softcap)
        hit = hit + jnp.where(ids == lane + (base_ref[0] + step * 256 + 128 * j), part, 0.0)
    sums[...] = total
    hits[...] = hit

    @pl.when(step == 3)
    def _():
        total_ref[...] = jnp.sum(total.T, axis=0, keepdims=True)
        target_ref[...] = jnp.sum(hit.T, axis=0, keepdims=True)


def forward(base, pieces, ids, head):
    whole = pl.BlockSpec((32, D), lambda n, *_: (0, 0))
    row = pl.BlockSpec((1, 256), lambda n, *_: (0, 0))
    return pl.pallas_call(
        forward_kernel,
        grid_spec=pltpu.PrefetchScalarGridSpec(
            num_scalar_prefetch=1,
            grid=(4,),
            in_specs=[whole] * 8
            + [
                pl.BlockSpec((256, 128), lambda n, *_: (0, 0)),
                pl.BlockSpec((D, 256), lambda n, *_: (0, n)),
            ],
            out_specs=[pl.BlockSpec((256, 256), lambda n, *_: (0, n)), row, row],
            scratch_shapes=[
                pltpu.VMEM((256, D), bf16),
                pltpu.VMEM((256, 128), f32),
                pltpu.VMEM((256, 128), f32),
            ],
        ),
        out_shape=[
            jax.ShapeDtypeStruct((256, WIDTH), f32),
            jax.ShapeDtypeStruct((1, 256), f32),
            jax.ShapeDtypeStruct((1, 256), f32),
        ],
        compiler_params=params(32),
        cost_estimate=cost(2 * 256 * D * WIDTH, 2 * D * WIDTH),
        name="forward",
    )(base, *pieces, ids, head)


def dlog_kernel(base_ref, low_ref, high_ref, log_ref, weight_ref, ids_ref, out_ref):
    step = pl.program_id(0)
    log_total = jnp.broadcast_to(log_ref[...], (128, 128)).T
    weight = weight_ref[...]
    ids = ids_ref[...]
    lane = lax.broadcasted_iota(jnp.int32, (128, 128), 1)

    def fill(capped_ref):
        for j in range(WIDTH // 128):
            spot = slice(128 * j, 128 * j + 128)
            capped = capped_ref[:, spot]
            prob = jnp.exp(capped - softcap - log_total)
            onehot = jnp.where(ids == lane + (base_ref[0] + 128 * j), 1.0, 0.0)
            ratio = capped / softcap
            out_ref[:, spot] = (weight * (prob - onehot) * (1.0 - ratio * ratio)).astype(bf16)

    @pl.when(step < 2)
    def _():
        fill(low_ref)

    @pl.when(step >= 2)
    def _():
        fill(high_ref)


def dlogits(base, low, high, log_total, weight, ids):
    column = pl.BlockSpec((128, 128), lambda n, *_: (n, 0))
    return pl.pallas_call(
        dlog_kernel,
        grid_spec=pltpu.PrefetchScalarGridSpec(
            num_scalar_prefetch=1,
            grid=(4,),
            in_specs=[
                pl.BlockSpec((128, WIDTH), lambda n, *_: (jnp.minimum(n, 1), 0)),
                pl.BlockSpec((128, WIDTH), lambda n, *_: (jnp.maximum(n - 2, 0), 0)),
                pl.BlockSpec((1, 128), lambda n, *_: (0, n)),
                column,
                column,
            ],
            out_specs=pl.BlockSpec((128, WIDTH), lambda n, *_: (n, 0)),
        ),
        out_shape=jax.ShapeDtypeStruct((512, WIDTH), bf16),
        compiler_params=params(24),
        cost_estimate=cost(512 * WIDTH * 16, 6 * 512 * WIDTH),
        name="dlog",
    )(base, low, high, log_total, weight, ids)


def product(dlog0, dlog1, head0, head1):
    rows = jnp.concatenate([dlog0[...], dlog1[...]], axis=0)
    features = jnp.concatenate([head0[...], head1[...]], axis=0)
    return lax.dot_general(rows, features, (((1,), (1,)), ((), ())), preferred_element_type=f32)


def mate_kernel(order_ref, dlog0, dlog1, head0, head1, out_ref):
    out_ref[...] = product(dlog0, dlog1, head0, head1).astype(bf16)


def mine_kernel(order_ref, dlog0, dlog1, head0, head1, got_ref, p_keep, p_send, q_keep, q_send, total):
    total[...] = product(dlog0, dlog1, head0, head1) + got_ref[...].astype(f32)
    for z in range(2):
        half = order_ref[8] if z == 0 else 1 - order_ref[8]
        for x in range(4):
            start = pl.multiple_of(half * 128, 128) + 32 * x
            (p_keep if x < 2 else p_send)[z, x % 2] = total[pl.ds(start, 16), :].astype(bf16)
            (q_keep if z == 0 else q_send)[x] = total[pl.ds(start + 16, 16), :].astype(bf16)


def hidden_specs(half, own):
    def rows(zr):
        return pl.BlockSpec((128, WIDTH), lambda n, *_: (2 * zr + 1 - own, 0))

    def block(i):
        return pl.BlockSpec((FEATURES, WIDTH), lambda n, order: (order[4 * half + 2 * n + i], 0))

    return [rows(0), rows(1), block(0), block(1)]


HALF_COST = 2 * 256 * WIDTH * D // 2


def mate_terms(half, order, dlog, head):
    return pl.pallas_call(
        mate_kernel,
        grid_spec=pltpu.PrefetchScalarGridSpec(
            num_scalar_prefetch=1,
            grid=(2,),
            in_specs=hidden_specs(half, 0),
            out_specs=pl.BlockSpec((256, 1152), lambda n, *_: (0, n)),
        ),
        out_shape=jax.ShapeDtypeStruct((256, 2304), bf16),
        compiler_params=params(32),
        cost_estimate=cost(HALF_COST, D * WIDTH),
        name="mate_terms",
    )(order, dlog, dlog, head, head)


def mine_terms(half, order, dlog, head, got):
    p_spec = pl.BlockSpec((2, 2, 16, 1152), lambda n, *_: (0, 0, 0, n))
    q_spec = pl.BlockSpec((4, 16, 1152), lambda n, *_: (0, 0, n))
    p_shape = jax.ShapeDtypeStruct((2, 2, 16, 2304), bf16)
    q_shape = jax.ShapeDtypeStruct((4, 16, 2304), bf16)
    return pl.pallas_call(
        mine_kernel,
        grid_spec=pltpu.PrefetchScalarGridSpec(
            num_scalar_prefetch=1,
            grid=(2,),
            in_specs=hidden_specs(half, 1) + [pl.BlockSpec((256, 1152), lambda n, *_: (0, n))],
            out_specs=[p_spec, p_spec, q_spec, q_spec],
            scratch_shapes=[pltpu.VMEM((256, 1152), f32)],
        ),
        out_shape=[p_shape, p_shape, q_shape, q_shape],
        compiler_params=params(32),
        cost_estimate=cost(HALF_COST, D * WIDTH),
        name="mine_terms",
    )(order, dlog, dlog, head, head, got)


def head_grad_kernel(*refs):
    pieces, (dlog_ref, out_ref) = refs[:16], refs[16:]
    rows = jnp.concatenate([piece[...] for piece in pieces], axis=0)
    out_ref[...] = lax.dot_general(
        rows, dlog_ref[...], (((0,), (0,)), ((), ())), preferred_element_type=f32
    ).astype(bf16)


def head_gradient(pieces, dlog):
    return pl.pallas_call(
        head_grad_kernel,
        grid=(9,),
        in_specs=[pl.BlockSpec((32, 512), lambda n: (0, n))] * 16
        + [pl.BlockSpec((512, WIDTH), lambda n: (0, 0))],
        out_specs=pl.BlockSpec((512, WIDTH), lambda n: (n, 0)),
        out_shape=jax.ShapeDtypeStruct((D, WIDTH), bf16),
        compiler_params=params(32),
        cost_estimate=cost(2 * 512 * WIDTH * D, 2 * D * WIDTH),
        name="head_gradient",
    )(*pieces, dlog)


def local(hidden, head, verdict_ids, row_weight):
    width = head.shape[1]
    dp = lax.axis_index("dp")
    vocab = lax.axis_index("vocab")
    core, x, zh = dp & 1, (dp >> 1) & 3, dp >> 3
    zl, y = vocab >> 2, vocab & 3
    zero = jnp.zeros_like(core)
    near = 1 + 2 * core
    far = 3 - 2 * core
    mine = jnp.stack([zero, near, far, zero + 2])
    mate = jnp.stack([zero, far, near, zero + 2])

    def ring(own):
        a1, a2 = send(own, X1), send(own, X2)
        return [own, a1, a2, send(a1, X2)]

    own_half = ring(hidden)
    other_half = ring(send(hidden, ZH))
    halves = [half + [send(piece, CORE) for piece in half] for half in (own_half, other_half)]
    blocks = jnp.concatenate(
        [
            ((zh ^ zr) << 3) | ((x ^ slots) << 1) | c
            for zr in (0, 1)
            for slots, c in ((mine, core), (mate, 1 - core))
        ]
    )
    place = blocks[:, None] == jnp.arange(16, dtype=blocks.dtype)[None, :]

    def to_local(whole):
        return jnp.sum(
            jnp.where(place[:, :, None], whole.reshape(1, 16, 32), jnp.zeros((), whole.dtype)), axis=1
        ).reshape(512)

    def to_whole(part):
        return jnp.sum(jnp.where(place[:, :, None], part.reshape(16, 1, 32), 0.0), axis=0)

    def order_of(slots, second):
        blocks_of = [((zl ^ zr) << 2) | (y ^ slots) for zr in (0, 1)]
        return jnp.concatenate(blocks_of + [jnp.stack([second])]).astype(jnp.int32)

    ids = jnp.broadcast_to(to_local(verdict_ids)[:, None], (512, 128))
    weight = jnp.broadcast_to(to_local(row_weight)[:, None], (512, 128))
    base = ((dp * 8 + vocab) * width).astype(jnp.int32).reshape(1)

    capped0, total0, target0 = forward(base, halves[0], ids[:256], head)
    capped1, total1, target1 = forward(base, halves[1], ids[256:], head)
    partial_total = to_whole(jnp.concatenate([total0, total1], axis=1))
    partial_target = to_whole(jnp.concatenate([target0, target1], axis=1))
    parcel = jnp.concatenate(
        [
            jnp.broadcast_to(partial_total.reshape(1, 512), (128, 512)),
            jnp.repeat(partial_target, 8, axis=0),
            jnp.zeros((128, 96), f32),
        ],
        axis=1,
    )
    arrived = lax.all_to_all(parcel.reshape(128, 1, 640), AXES, 0, 0, tiled=True)
    sums = jnp.sum(arrived, axis=(0, 1))
    log_total = jnp.log(sums[:512])
    target = sums[512:544]
    own_log = lax.dynamic_slice_in_dim(log_total, dp * 32, 32, 0)
    logprob = target - softcap - own_log
    dlog = dlogits(base, capped0, capped1, to_local(log_total).reshape(1, 512), weight, ids)

    mate_order = order_of(mate, zero)
    mine_order = order_of(mine, zero)
    turned_order = order_of(mine, core)
    got_a = send(mate_terms(0, mate_order, dlog, head), CORE)
    got_b = send(mate_terms(1, mate_order, dlog, head), CORE)
    pa_keep, pa_send, qa_keep, qa_send = mine_terms(0, mine_order, dlog, head, got_a)
    pb_keep, pb_send, qb_keep, qb_send = mine_terms(1, turned_order, dlog, head, got_b)

    def add(a, b):
        return (a.astype(f32) + b.astype(f32)).astype(bf16)

    pa = add(pa_keep, send(pa_send, X2))
    qa_got = send(qa_send, Z2)
    pb = add(pb_keep, send(pb_send, X2))
    qb_got = send(qb_send, Z2)
    q0, q1 = add(qa_keep, qb_got), add(qb_keep, qa_got)
    p_got = send(jnp.concatenate([pa[:, 1], pb[:, 1]], axis=0), X1)
    q = add(q0, send(q1, Z1))
    pa = add(pa[:, 0], p_got[:2])
    pb = add(pb[:, 0], p_got[2:])
    p_got = send(jnp.stack([pb[1], pa[1]]), Z2)
    q = add(q[:2], send(q[2:], X2))
    p0, p1 = add(pa[0], p_got[0]), add(pb[0], p_got[1])
    p = add(p0, send(p1, Z1))
    q = add(q[0], send(q[1], X1))
    pq = jnp.concatenate([p, q], axis=0)
    pq = add(pq[:, :1152], send(pq[:, 1152:], Y2))
    hidden_grad = add(pq[:, :576], send(pq[:, 576:], Y1))

    head_grad = head_gradient(halves[0] + halves[1], dlog)
    return (logprob, head_grad, hidden_grad)


def solution(mesh):
    in_specs = (P("dp", None), P(None, ("dp", "vocab")), P(), P())
    out_specs = (P("dp"), P(None, ("dp", "vocab")), P("dp", "vocab"))
    return jax.shard_map(local, mesh=mesh, in_specs=in_specs, out_specs=out_specs, check_vma=False)
```

time: 164 us -> 148 us (0.902)
  matrix products: 42.3 us -> 0 us
  Pallas kernels: 0 us -> 33.2 us
  local copies, waits for them, and re-layouts: 42.5 us -> 24.1 us
  waiting for transfers between devices: 30.9 us -> 44.6 us
  other arithmetic: 9.2 us -> 3.91 us
  starting transfers between devices: 37.5 us -> 39.4 us
    dot_general x5 -> x0, matrix products: 42.3 us -> none  [the longest x2 22.9 us: terms(): lax.dot_general(rows, ordered, (((1,), (1,)), ((), ())), preferred_elemen...]
    pallas_call x0 -> x8, Pallas kernels: none -> 33.2 us  [the longest x2 11 us: forward(): pl.pallas_call(forward_kernel, grid_spec=pltpu.PrefetchScalarGridSpec(num...]
    gather x2 -> x0, local copies, waits for them, and re-layouts: 18 us -> none  [terms(): ordered = head_blocks[feature_order(slots)].reshape(4608, width)]
    all_to_all x1, waiting for transfers between devices: 1.99 us -> 11.2 us  [local(): lax.all_to_all(parcel.reshape(128, 1, 640), AXES, 0, 0, tiled=True)]
    unnamed x27 -> x72, local copies, waits for them, and re-layouts: 13.2 us -> 20.2 us
    ppermute x26 -> x29, waiting for transfers between devices: 28.9 us -> 33.4 us  [send(): return lax.ppermute(array, AXES, partner)]
    slice x3 -> x5, local copies, waits for them, and re-layouts: 4.45 us -> 0.17 us  [the longest x2 0.08 us: local(): capped0, total0, target0 = forward(base, halves[0], ids[:256], head)]
    reshape x1 -> x0, local copies, waits for them, and re-layouts: 2.63 us -> none  [local(): summed = add(for_me, got).reshape(2, 4, 32, 2, 2304)]
  transfers between devices with their start and end apart: 27 -> 30, of which waited for: 12 -> 12; matrix products, arithmetic and copies ran while one was open for 32% -> 3% of each run, Pallas kernels for 0% -> 16%
where the time goes in v2:
time: 148 us; the launch traced here: 147 us
  waiting for transfers between devices  44.6 us (30%)
  starting transfers between devices  39.4 us (27%)
  Pallas kernels  33.2 us (22%)
  local copies, waits for them, and re-layouts  24.1 us (16%)
  other arithmetic  3.91 us (3%)
    ppermute x29, waiting for transfers between devices, send(): return lax.ppermute(array, AXES, partner)  33.4 us
    ppermute x29, starting transfers between devices, send(): return lax.ppermute(array, AXES, partner)  29 us
    unnamed x72, local copies, waits for them, and re-layouts  20.2 us
    all_to_all x1, waiting for transfers between devices, local(): lax.all_to_all(parcel.reshape(128, 1, 640), AXES, 0, 0, tiled=True)  11.2 us
    pallas_call x2, Pallas kernels, forward(): pl.pallas_call(forward_kernel, grid_spec=pltpu.PrefetchScalarGridSpec(num...  11 us
    all_to_all x1, starting transfers between devices, local(): lax.all_to_all(parcel.reshape(128, 1, 640), AXES, 0, 0, tiled=True)  10.4 us
    pallas_call x1, Pallas kernels, head_gradient(): pl.pallas_call(head_grad_kernel, grid=(9,), in_specs=[pl.BlockSpec((32, 5...  10.1 us
    pallas_call x2, Pallas kernels, mine_terms(): pl.pallas_call(mine_kernel, grid_spec=pltpu.PrefetchScalarGridSpec(num_sc...  5.99 us
  transfers between devices with their start and end apart: 30, of which 12 were waited for; matrix products, arithmetic and copies ran while one was open for 3% of the time, Pallas kernels for 16%

profile of v2, /device:TPU:0, one launch (start us, length us, event | category | flops | bytes accessed | tf_op | source)
XLA Modules:
  0.0 146.5 jit_solution(16803274011000922362)
XLA Ops:
  0.6 4.2 %collective-permute-start.7 = (bf16[32,4608]{1,0:T(8,128)(2,1)}, bf16[32,4608]{1,0:T(8,128)(2,1)S(1)}, u32[]{:S(2)}, u32[]{:S(2)}) collective-permute-start(bf16[32,4608]{1,0:T(8,128)(2,1)} %refs_0_.3), channel_id=1, source_target_pairs={{0,68},{1,69},{2,70},{3,71},{4,64},{5,65},{6,66},{7,67},{8,76},{9,... | collective-permute-start | bytes 884744 | tf_op jit(solution)/shard_map/ppermute | solution.py:31
  4.8 1.5 %collective-permute-start = (bf16[32,4608]{1,0:T(8,128)(2,1)}, bf16[32,4608]{1,0:T(8,128)(2,1)S(1)}, u32[]{:S(2)}, u32[]{:S(2)}) collective-permute-start(bf16[32,4608]{1,0:T(8,128)(2,1)} %refs_0_.3), channel_id=1, source_target_pairs={{0,16},{1,17},{2,18},{3,19},{4,20},{5,21},{6,22},{7,23},{8,56},{9,... | collective-permute-start | bytes 884744 | tf_op jit(solution)/shard_map/ppermute | solution.py:31
  6.3 2.1 %collective-permute-start.1 = (bf16[32,4608]{1,0:T(8,128)(2,1)}, bf16[32,4608]{1,0:T(8,128)(2,1)S(1)}, u32[]{:S(2)}, u32[]{:S(2)}) collective-permute-start(bf16[32,4608]{1,0:T(8,128)(2,1)} %refs_0_.3), channel_id=1, source_target_pairs={{0,48},{1,49},{2,50},{3,51},{4,52},{5,53},{6,54},{7,55},{8,24},{9,... | collective-permute-start | bytes 884744 | tf_op jit(solution)/shard_map/ppermute | solution.py:31
  9.3 2.7 %collective-permute-done.7.refs_0_.refs_8_ = bf16[32,4608]{1,0:T(8,128)(2,1)S(1)} collective-permute-done((bf16[32,4608]{1,0:T(8,128)(2,1)}, bf16[32,4608]{1,0:T(8,128)(2,1)S(1)}, u32[]{:S(2)}, u32[]{:S(2)}) %collective-permute-start.7) | collective-permute-done | bytes 294944 | tf_op jit(solution)/shard_map/ppermute | solution.py:31
  12.1 1.5 %collective-permute-start.8 = (bf16[32,4608]{1,0:T(8,128)(2,1)S(1)}, bf16[32,4608]{1,0:T(8,128)(2,1)S(1)}, u32[]{:S(2)}, u32[]{:S(2)}) collective-permute-start(bf16[32,4608]{1,0:T(8,128)(2,1)S(1)} %collective-permute-done.7.refs_0_.refs_8_), channel_id=1, source_target_pairs={{0,16},{1,17},{2,18},{3,19},{4,20},{5,21},{6,22},{7,23},{8,56},{9,... | collective-permute-start | bytes 884744 | tf_op jit(solution)/shard_map/ppermute | solution.py:31
  13.9 2.5 %collective-permute-start.2 = (bf16[32,4608]{1,0:T(8,128)(2,1)S(1)}, bf16[32,4608]{1,0:T(8,128)(2,1)S(1)}, u32[]{:S(2)}, u32[]{:S(2)}) collective-permute-start(bf16[32,4608]{1,0:T(8,128)(2,1)S(1)} %collective-permute-done.refs_1_), channel_id=1, source_target_pairs={{0,48},{1,49},{2,50},{3,51},{4,52},{5,53},{6,54},{7,55},{8,24},{9,... | collective-permute-start | bytes 884744 | tf_op jit(solution)/shard_map/ppermute | solution.py:31
  17.8 3.3 %collective-permute-done.8.refs_1_.refs_9_ = bf16[32,4608]{1,0:T(8,128)(2,1)S(1)} collective-permute-done((bf16[32,4608]{1,0:T(8,128)(2,1)S(1)}, bf16[32,4608]{1,0:T(8,128)(2,1)S(1)}, u32[]{:S(2)}, u32[]{:S(2)}) %collective-permute-start.8) | collective-permute-done | bytes 294944 | tf_op jit(solution)/shard_map/ppermute | solution.py:31
  21.1 3.6 %collective-permute-start.10 = (bf16[32,4608]{1,0:T(8,128)(2,1)S(1)}, bf16[32,4608]{1,0:T(8,128)(2,1)}, u32[]{:S(2)}, u32[]{:S(2)}) collective-permute-start(bf16[32,4608]{1,0:T(8,128)(2,1)S(1)} %collective-permute-done.8.refs_1_.refs_9_), channel_id=1, source_target_pairs={{0,48},{1,49},{2,50},{3,51},{4,52},{5,53},{6,54},{7,55},{8,24},{9,... | collective-permute-start | bytes 884744 | tf_op jit(solution)/shard_map/ppermute | solution.py:31
  27.5 2.0 %collective-permute-done.10.refs_3_.refs_11_ = bf16[32,4608]{1,0:T(8,128)(2,1)} collective-permute-done((bf16[32,4608]{1,0:T(8,128)(2,1)S(1)}, bf16[32,4608]{1,0:T(8,128)(2,1)}, u32[]{:S(2)}, u32[]{:S(2)}) %collective-permute-start.10) | collective-permute-done | bytes 294944 | tf_op jit(solution)/shard_map/ppermute | solution.py:31
  31.3 3.7 %copy-done = bf16[4608,1024]{1,0:T(8,128)(2,1)S(1)} copy-done((bf16[4608,1024]{1,0:T(8,128)(2,1)S(1)}, bf16[4608,1024]{1,0:T(8,128)(2,1)}, u32[]{:S(2)}) %copy-start) | copy-done | bytes 9437208
  38.8 5.0 %forward.2 = (f32[256,1024]{1,0:T(8,128)S(1)}, f32[1,256]{1,0:T(1,128)S(1)}, f32[1,256]{1,0:T(1,128)S(1)}) custom-call(s32[1]{0:T(128)} %bitcast.2.base_ref, bf16[32,4608]{1,0:T(8,128)(2,1)S(1)} %copy-done.4, bf16[32,4608]{1,0:T(8,128)(2,1)S(1)} %collective-permute-done.refs_1_, bf16[32,4608]{1,0:T(8,128)(2,1)S(1)} %collective-permute-done.1.refs_2_, ...), custom_call_target="tpu_custom_call" | custom-call | flops 2415919104 | bytes 9437184 | tf_op jit(solution)/shard_map/forward/pallas_call | solution.py:76
  45.0 6.0 %forward.3 = (f32[256,1024]{1,0:T(8,128)S(1)}, f32[1,256]{1,0:T(1,128)S(1)}, f32[1,256]{1,0:T(1,128)S(1)}) custom-call(s32[1]{0:T(128)} %bitcast.2.base_ref, bf16[32,4608]{1,0:T(8,128)(2,1)S(1)} %collective-permute-done.7.refs_0_.refs_8_, bf16[32,4608]{1,0:T(8,128)(2,1)S(1)} %collective-permute-done.8.refs_1_.refs_9_, bf16[32,4608]{1,0:T(8,128)(2,1)S(1)} %copy-done.19, ...), custom_call_target="tpu_custom_call" | custom-call | flops 2415919104 | bytes 9437184 | tf_op jit(solution)/shard_map/forward/pallas_call | solution.py:76
  52.4 10.4 %all-to-all-start = ((f32[128,1,640]{2,1,0:T(1,128)}), f32[128,1,640]{2,1,0:T(1,128)S(1)}, u32[]{:S(2)}, u32[]{:S(2)}) async-start(f32[128,1,640]{2,1,0:T(1,128)} %reshape.81), calls=%async_computation | async-start | bytes 655360 | tf_op jit(solution)/shard_map/all_to_all | solution.py:300
  63.1 11.2 %all-to-all-done = f32[128,1,640]{2,1,0:T(1,128)S(1)} async-done(((f32[128,1,640]{2,1,0:T(1,128)}), f32[128,1,640]{2,1,0:T(1,128)S(1)}, u32[]{:S(2)}, u32[]{:S(2)}) %all-to-all-start) | async-done | bytes 327712 | tf_op jit(solution)/shard_map/all_to_all | solution.py:300
  75.1 1.3 dlog.1.refs_16_.dlog0.dlog1
  76.4 3.7 %copy-done.2 = bf16[4608,1024]{1,0:T(8,128)(2,1)S(1)} copy-done((bf16[4608,1024]{1,0:T(8,128)(2,1)S(1)}, bf16[4608,1024]{1,0:T(8,128)(2,1)}, u32[]{:S(2)}) %copy-start.2) | copy-done | bytes 9437208
  80.1 2.4 %mate_terms.2 = bf16[256,2304]{1,0:T(8,128)(2,1)S(1)} custom-call(s32[9]{0:T(128)S(1)} %pad_add_fusion.4.order_ref, bf16[512,1024]{1,0:T(8,128)(2,1)S(1)} %dlog.1.refs_16_.dlog0.dlog1, bf16[512,1024]{1,0:T(8,128)(2,1)S(1)} %dlog.1.refs_16_.dlog0.dlog1, bf16[4608,1024]{1,0:T(8,128)(2,1)S(1)} %copy-done.2, bf16[4608,1024]{1,0:T(8,128)(2,1)S(1)} %copy-done.2), custom_call_target="tpu_custom_call" | custom-call | flops 1207959552 | bytes 4718592 | tf_op jit(solution)/shard_map/mate_terms/pallas_call | solution.py:186
  82.6 2.4 %mate_terms.3 = bf16[256,2304]{1,0:T(8,128)(2,1)S(1)} custom-call(s32[9]{0:T(128)S(1)} %pad_add_fusion.4.order_ref, bf16[512,1024]{1,0:T(8,128)(2,1)S(1)} %dlog.1.refs_16_.dlog0.dlog1, bf16[512,1024]{1,0:T(8,128)(2,1)S(1)} %dlog.1.refs_16_.dlog0.dlog1, bf16[4608,1024]{1,0:T(8,128)(2,1)S(1)} %copy-done.2, bf16[4608,1024]{1,0:T(8,128)(2,1)S(1)} %copy-done.2), custom_call_target="tpu_custom_call" | custom-call | flops 1207959552 | bytes 4718592 | tf_op jit(solution)/shard_map/mate_terms/pallas_call | solution.py:186
  85.7 3.3 %mine_terms.2 = (bf16[2,2,16,2304]{3,2,1,0:T(8,128)(2,1)S(1)}, bf16[2,2,16,2304]{3,2,1,0:T(8,128)(2,1)S(1)}, bf16[4,16,2304]{2,1,0:T(8,128)(2,1)S(1)}, bf16[4,16,2304]{2,1,0:T(8,128)(2,1)}) custom-call(s32[9]{0:T(128)S(1)} %get-tuple-element.43.order_ref, bf16[512,1024]{1,0:T(8,128)(2,1)S(1)} %dlog.1.refs_16_.dlog0.dlog1, ...), custom_call_target="tpu_custom_call" | custom-call | flops 1207959552 | bytes 4718592 | tf_op jit(solution)/shard_map/mine_terms/pallas_call | solution.py:206
  92.1 3.7 %copy-done.3 = bf16[4608,1024]{1,0:T(8,128)(2,1)S(1)} copy-done((bf16[4608,1024]{1,0:T(8,128)(2,1)S(1)}, bf16[4608,1024]{1,0:T(8,128)(2,1)}, u32[]{:S(2)}) %copy-start.3) | copy-done | bytes 9437208
  95.8 2.7 %mine_terms.3 = (bf16[2,2,16,2304]{3,2,1,0:T(8,128)(2,1)S(1)}, bf16[2,2,16,2304]{3,2,1,0:T(8,128)(2,1)S(1)}, bf16[4,16,2304]{2,1,0:T(8,128)(2,1)S(1)}, bf16[4,16,2304]{2,1,0:T(8,128)(2,1)S(1)}) custom-call(s32[9]{0:T(128)S(1)} %get-tuple-element.42.order_ref, bf16[512,1024]{1,0:T(8,128)(2,1)S(1)} %dlog.1.refs_16_.dlog0.dlog1, ...), custom_call_target="tpu_custom_call" | custom-call | flops 1207959552 | bytes 4718592 | tf_op jit(solution)/shard_map/mine_terms/pallas_call | solution.py:206
  98.4 2.4 %collective-permute-start.22 = (bf16[4,16,2304]{2,1,0:T(8,128)(2,1)S(1)}, bf16[4,16,2304]{2,1,0:T(8,128)(2,1)S(1)}, u32[]{:S(2)}, u32[]{:S(2)}) collective-permute-start(bf16[4,16,2304]{2,1,0:T(8,128)(2,1)S(1)} %get-tuple-element.28), channel_id=1, source_target_pairs={{0,68},{1,69},{2,70},{3,71},{4,64},{5,65},{6,66},{7,67},{8,12},{9,... | collective-permute-start | bytes 884744 | tf_op jit(solution)/shard_map/ppermute | solution.py:31
  101.9 2.4 %collective-permute-start.16 = (bf16[2,2,16,2304]{3,2,0,1:T(8,128)(2,1)S(1)}, bf16[2,2,16,2304]{3,2,0,1:T(8,128)(2,1)S(1)}, u32[]{:S(2)}, u32[]{:S(2)}) collective-permute-start(bf16[2,2,16,2304]{3,2,0,1:T(8,128)(2,1)S(1)} %copy.16), channel_id=1, source_target_pairs={{0,48},{1,49},{2,50},{3,51},{4,52},{5,53},{6,54},{7,55},{8,24},{9,... | collective-permute-start | bytes 884744 | tf_op jit(solution)/shard_map/ppermute | solution.py:31
  104.3 1.0 add_convert_fusion.1
  105.4 3.4 %collective-permute-done.18 = bf16[2,2,16,2304]{3,2,0,1:T(8,128)(2,1)S(1)} collective-permute-done((bf16[2,2,16,2304]{3,2,0,1:T(8,128)(2,1)S(1)}, bf16[2,2,16,2304]{3,2,0,1:T(8,128)(2,1)S(1)}, u32[]{:S(2)}, u32[]{:S(2)}) %collective-permute-start.18) | collective-permute-done | bytes 294944 | tf_op jit(solution)/shard_map/ppermute | solution.py:31
  109.0 3.1 %collective-permute-done.16 = bf16[2,2,16,2304]{3,2,0,1:T(8,128)(2,1)S(1)} collective-permute-done((bf16[2,2,16,2304]{3,2,0,1:T(8,128)(2,1)S(1)}, bf16[2,2,16,2304]{3,2,0,1:T(8,128)(2,1)S(1)}, u32[]{:S(2)}, u32[]{:S(2)}) %collective-permute-start.16) | collective-permute-done | bytes 294944 | tf_op jit(solution)/shard_map/ppermute | solution.py:31
  113.4 5.5 %collective-permute-done.19 = bf16[4,16,2304]{2,1,0:T(8,128)(2,1)S(1)} collective-permute-done((bf16[4,16,2304]{2,1,0:T(8,128)(2,1)S(1)}, bf16[4,16,2304]{2,1,0:T(8,128)(2,1)S(1)}, u32[]{:S(2)}, u32[]{:S(2)}) %collective-permute-start.19) | collective-permute-done | bytes 294944 | tf_op jit(solution)/shard_map/ppermute | solution.py:31
  120.6 5.2 %collective-permute-done.20 = bf16[2,16,2304]{2,1,0:T(8,128)(2,1)S(1)} collective-permute-done((bf16[2,16,2304]{2,1,0:T(8,128)(2,1)S(1)}, bf16[2,16,2304]{2,1,0:T(8,128)(2,1)S(1)}, u32[]{:S(2)}, u32[]{:S(2)}) %collective-permute-start.20) | collective-permute-done | bytes 147488 | tf_op jit(solution)/shard_map/ppermute | solution.py:31
  125.9 4.3 %collective-permute-done.21 = bf16[16,2304]{1,0:T(8,128)(2,1)S(1)} collective-permute-done((bf16[16,2304]{1,0:T(8,128)(2,1)S(1)}, bf16[16,2304]{1,0:T(8,128)(2,1)S(1)}, u32[]{:S(2)}, u32[]{:S(2)}) %collective-permute-start.21) | collective-permute-done | bytes 73760 | tf_op jit(solution)/shard_map/ppermute | solution.py:31
  130.3 1.3 collective-permute-start.27
  131.6 10.1 %head_gradient.1 = bf16[4608,1024]{1,0:T(8,128)(2,1)} custom-call(bf16[32,4608]{1,0:T(8,128)(2,1)S(1)} %copy-done.5, bf16[32,4608]{1,0:T(8,128)(2,1)S(1)} %copy-done.9, bf16[32,4608]{1,0:T(8,128)(2,1)S(1)} %copy-done.11, bf16[32,4608]{1,0:T(8,128)(2,1)S(1)} %copy-done.17, bf16[32,4608]{1,0:T(8,128)(2,1)S(1)} %copy-done.13, bf16[32,4608]{1,0:T(8,128)(2,1)S(1)} %copy-done.23, ...), custom_call_target="tpu_custom_call" | custom-call | flops 4831838208 | bytes 9437184 | tf_op jit(solution)/shard_map/head_gradient/pallas_call | solution.py:231
  142.5 3.4 %collective-permute-done.28 = bf16[32,576]{1,0:T(8,128)(2,1)S(1)} collective-permute-done((bf16[32,576]{1,0:T(8,128)(2,1)S(1)}, bf16[32,576]{1,0:T(8,128)(2,1)S(1)}, u32[]{:S(2)}, u32[]{:S(2)}) %collective-permute-start.28) | collective-permute-done | bytes 36896 | tf_op jit(solution)/shard_map/ppermute | solution.py:31
  (168 shorter events, 24.1 us)
Async XLA Ops:
  0.6 11.4 %collective-permute-start.7 = (bf16[32,4608]{1,0:T(8,128)(2,1)}, bf16[32,4608]{1,0:T(8,128)(2,1)S(1)}, u32[]{:S(2)}, u32[]{:S(2)}) collective-permute-start(bf16[32,4608]{1,0:T(8,128)(2,1)} %refs_0_.3), channel_id=1, source_target_pairs={{0,68},{1,69},{2,70},{3,71},{4,64},{5,65},{6,66},{7,67},{8,76},{9,... | collective-permute-start | bytes 884744 | tf_op jit(solution)/shard_map/ppermute | solution.py:31
  4.8 9.1 %collective-permute-start = (bf16[32,4608]{1,0:T(8,128)(2,1)}, bf16[32,4608]{1,0:T(8,128)(2,1)S(1)}, u32[]{:S(2)}, u32[]{:S(2)}) collective-permute-start(bf16[32,4608]{1,0:T(8,128)(2,1)} %refs_0_.3), channel_id=1, source_target_pairs={{0,16},{1,17},{2,18},{3,19},{4,20},{5,21},{6,22},{7,23},{8,56},{9,... | collective-permute-start | bytes 884744 | tf_op jit(solution)/shard_map/ppermute | solution.py:31
  6.3 10.9 %collective-permute-start.1 = (bf16[32,4608]{1,0:T(8,128)(2,1)}, bf16[32,4608]{1,0:T(8,128)(2,1)S(1)}, u32[]{:S(2)}, u32[]{:S(2)}) collective-permute-start(bf16[32,4608]{1,0:T(8,128)(2,1)} %refs_0_.3), channel_id=1, source_target_pairs={{0,48},{1,49},{2,50},{3,51},{4,52},{5,53},{6,54},{7,55},{8,24},{9,... | collective-permute-start | bytes 884744 | tf_op jit(solution)/shard_map/ppermute | solution.py:31
  8.4 8.9 %collective-permute-start.3 = (bf16[32,4608]{1,0:T(8,128)(2,1)}, bf16[32,4608]{1,0:T(8,128)(2,1)S(1)}, u32[]{:S(2)}, u32[]{:S(2)}) collective-permute-start(bf16[32,4608]{1,0:T(8,128)(2,1)} %refs_0_.3), channel_id=1, source_target_pairs={{0,8},{1,9},{2,10},{3,11},{4,12},{5,13},{6,14},{7,15},{8,0},{9,1},... | collective-permute-start | bytes 884744 | tf_op jit(solution)/shard_map/ppermute | solution.py:31
  12.1 31.9 %copy-start.6 = (bf16[32,4608]{1,0:T(8,128)(2,1)}, bf16[32,4608]{1,0:T(8,128)(2,1)S(1)}, u32[]{:S(2)}) copy-start(bf16[32,4608]{1,0:T(8,128)(2,1)S(1)} %collective-permute-done.7.refs_0_.refs_8_) | copy-start | bytes 884740
  12.1 9.0 %collective-permute-start.8 = (bf16[32,4608]{1,0:T(8,128)(2,1)S(1)}, bf16[32,4608]{1,0:T(8,128)(2,1)S(1)}, u32[]{:S(2)}, u32[]{:S(2)}) collective-permute-start(bf16[32,4608]{1,0:T(8,128)(2,1)S(1)} %collective-permute-done.7.refs_0_.refs_8_), channel_id=1, source_target_pairs={{0,16},{1,17},{2,18},{3,19},{4,20},{5,21},{6,22},{7,23},{8,56},{9,... | collective-permute-start | bytes 884744 | tf_op jit(solution)/shard_map/ppermute | solution.py:31
  13.9 29.9 %copy-start.8 = (bf16[32,4608]{1,0:T(8,128)(2,1)}, bf16[32,4608]{1,0:T(8,128)(2,1)S(1)}, u32[]{:S(2)}) copy-start(bf16[32,4608]{1,0:T(8,128)(2,1)S(1)} %collective-permute-done.refs_1_) | copy-start | bytes 884740
  13.9 10.8 %collective-permute-start.2 = (bf16[32,4608]{1,0:T(8,128)(2,1)S(1)}, bf16[32,4608]{1,0:T(8,128)(2,1)S(1)}, u32[]{:S(2)}, u32[]{:S(2)}) collective-permute-start(bf16[32,4608]{1,0:T(8,128)(2,1)S(1)} %collective-permute-done.refs_1_), channel_id=1, source_target_pairs={{0,48},{1,49},{2,50},{3,51},{4,52},{5,53},{6,54},{7,55},{8,24},{9,... | collective-permute-start | bytes 884744 | tf_op jit(solution)/shard_map/ppermute | solution.py:31
  16.5 8.5 %collective-permute-start.9 = (bf16[32,4608]{1,0:T(8,128)(2,1)S(1)}, bf16[32,4608]{1,0:T(8,128)(2,1)S(1)}, u32[]{:S(2)}, u32[]{:S(2)}) collective-permute-start(bf16[32,4608]{1,0:T(8,128)(2,1)S(1)} %collective-permute-done.7.refs_0_.refs_8_), channel_id=1, source_target_pairs={{0,48},{1,49},{2,50},{3,51},{4,52},{5,53},{6,54},{7,55},{8,24},{9,... | collective-permute-start | bytes 884744 | tf_op jit(solution)/shard_map/ppermute | solution.py:31
  17.3 8.3 %collective-permute-start.4 = (bf16[32,4608]{1,0:T(8,128)(2,1)S(1)}, bf16[32,4608]{1,0:T(8,128)(2,1)S(1)}, u32[]{:S(2)}, u32[]{:S(2)}) collective-permute-start(bf16[32,4608]{1,0:T(8,128)(2,1)S(1)} %collective-permute-done.refs_1_), channel_id=1, source_target_pairs={{0,8},{1,9},{2,10},{3,11},{4,12},{5,13},{6,14},{7,15},{8,0},{9,1},... | collective-permute-start | bytes 884744 | tf_op jit(solution)/shard_map/ppermute | solution.py:31
  17.3 9.0 %collective-permute-start.5 = (bf16[32,4608]{1,0:T(8,128)(2,1)S(1)}, bf16[32,4608]{1,0:T(8,128)(2,1)S(1)}, u32[]{:S(2)}, u32[]{:S(2)}) collective-permute-start(bf16[32,4608]{1,0:T(8,128)(2,1)S(1)} %collective-permute-done.1.refs_2_), channel_id=1, source_target_pairs={{0,8},{1,9},{2,10},{3,11},{4,12},{5,13},{6,14},{7,15},{8,0},{9,1},... | collective-permute-start | bytes 884744 | tf_op jit(solution)/shard_map/ppermute | solution.py:31
  21.1 8.4 %collective-permute-start.10 = (bf16[32,4608]{1,0:T(8,128)(2,1)S(1)}, bf16[32,4608]{1,0:T(8,128)(2,1)}, u32[]{:S(2)}, u32[]{:S(2)}) collective-permute-start(bf16[32,4608]{1,0:T(8,128)(2,1)S(1)} %collective-permute-done.8.refs_1_.refs_9_), channel_id=1, source_target_pairs={{0,48},{1,49},{2,50},{3,51},{4,52},{5,53},{6,54},{7,55},{8,24},{9,... | collective-permute-start | bytes 884744 | tf_op jit(solution)/shard_map/ppermute | solution.py:31
  24.7 5.7 %collective-permute-start.6 = (bf16[32,4608]{1,0:T(8,128)(2,1)S(1)}, bf16[32,4608]{1,0:T(8,128)(2,1)S(1)}, u32[]{:S(2)}, u32[]{:S(2)}) collective-permute-start(bf16[32,4608]{1,0:T(8,128)(2,1)S(1)} %collective-permute-done.2.refs_3_), channel_id=1, source_target_pairs={{0,8},{1,9},{2,10},{3,11},{4,12},{5,13},{6,14},{7,15},{8,0},{9,1},... | collective-permute-start | bytes 884744 | tf_op jit(solution)/shard_map/ppermute | solution.py:31
  25.0 18.8 %collective-permute-start.11 = (bf16[32,4608]{1,0:T(8,128)(2,1)S(1)}, bf16[32,4608]{1,0:T(8,128)(2,1)}, u32[]{:S(2)}, u32[]{:S(2)}) collective-permute-start(bf16[32,4608]{1,0:T(8,128)(2,1)S(1)} %collective-permute-done.7.refs_0_.refs_8_), channel_id=1, source_target_pairs={{0,8},{1,9},{2,10},{3,11},{4,12},{5,13},{6,14},{7,15},{8,0},{9,1},... | collective-permute-start | bytes 884744 | tf_op jit(solution)/shard_map/ppermute | solution.py:31
  26.2 17.6 %collective-permute-start.12 = (bf16[32,4608]{1,0:T(8,128)(2,1)S(1)}, bf16[32,4608]{1,0:T(8,128)(2,1)}, u32[]{:S(2)}, u32[]{:S(2)}) collective-permute-start(bf16[32,4608]{1,0:T(8,128)(2,1)S(1)} %collective-permute-done.8.refs_1_.refs_9_), channel_id=1, source_target_pairs={{0,8},{1,9},{2,10},{3,11},{4,12},{5,13},{6,14},{7,15},{8,0},{9,1},... | collective-permute-start | bytes 884744 | tf_op jit(solution)/shard_map/ppermute | solution.py:31
  27.0 16.9 %collective-permute-start.13 = (bf16[32,4608]{1,0:T(8,128)(2,1)S(1)}, bf16[32,4608]{1,0:T(8,128)(2,1)}, u32[]{:S(2)}, u32[]{:S(2)}) collective-permute-start(bf16[32,4608]{1,0:T(8,128)(2,1)S(1)} %collective-permute-done.9.refs_2_.refs_10_), channel_id=1, source_target_pairs={{0,8},{1,9},{2,10},{3,11},{4,12},{5,13},{6,14},{7,15},{8,0},{9,1},... | collective-permute-start | bytes 884744 | tf_op jit(solution)/shard_map/ppermute | solution.py:31
  29.4 14.5 %collective-permute-start.14 = (bf16[32,4608]{1,0:T(8,128)(2,1)}, bf16[32,4608]{1,0:T(8,128)(2,1)}, u32[]{:S(2)}, u32[]{:S(2)}) collective-permute-start(bf16[32,4608]{1,0:T(8,128)(2,1)} %collective-permute-done.10.refs_3_.refs_11_), channel_id=1, source_target_pairs={{0,8},{1,9},{2,10},{3,11},{4,12},{5,13},{6,14},{7,15},{8,0},{9,1},... | collective-permute-start | bytes 884744 | tf_op jit(solution)/shard_map/ppermute | solution.py:31
  52.4 21.8 %all-to-all-start = ((f32[128,1,640]{2,1,0:T(1,128)}), f32[128,1,640]{2,1,0:T(1,128)S(1)}, u32[]{:S(2)}, u32[]{:S(2)}) async-start(f32[128,1,640]{2,1,0:T(1,128)} %reshape.81), calls=%async_computation | async-start | bytes 655360 | tf_op jit(solution)/shard_map/all_to_all | solution.py:300
  82.5 3.2 %collective-permute-start.15 = (bf16[256,2304]{1,0:T(8,128)(2,1)S(1)}, bf16[256,2304]{1,0:T(8,128)(2,1)S(1)}, u32[]{:S(2)}, u32[]{:S(2)}) collective-permute-start(bf16[256,2304]{1,0:T(8,128)(2,1)S(1)} %mate_terms.2), channel_id=1, source_target_pairs={{0,8},{1,9},{2,10},{3,11},{4,12},{5,13},{6,14},{7,15},{8,0},{9,1},... | collective-permute-start | bytes 3538952 | tf_op jit(solution)/shard_map/ppermute | solution.py:31
  85.0 7.1 %collective-permute-start.17 = (bf16[256,2304]{1,0:T(8,128)(2,1)S(1)}, bf16[256,2304]{1,0:T(8,128)(2,1)S(1)}, u32[]{:S(2)}, u32[]{:S(2)}) collective-permute-start(bf16[256,2304]{1,0:T(8,128)(2,1)S(1)} %mate_terms.3), channel_id=1, source_target_pairs={{0,8},{1,9},{2,10},{3,11},{4,12},{5,13},{6,14},{7,15},{8,0},{9,1},... | collective-permute-start | bytes 3538952 | tf_op jit(solution)/shard_map/ppermute | solution.py:31
  91.1 13.2 %collective-permute-start.23 = (bf16[4,16,2304]{2,1,0:T(8,128)(2,1)}, bf16[4,16,2304]{2,1,0:T(8,128)(2,1)}, u32[]{:S(2)}, u32[]{:S(2)}) collective-permute-start(bf16[4,16,2304]{2,1,0:T(8,128)(2,1)} %get-tuple-element.30), channel_id=1, source_target_pairs={{0,68},{1,69},{2,70},{3,71},{4,64},{5,65},{6,66},{7,67},{8,12},{9,... | collective-permute-start | bytes 884744 | tf_op jit(solution)/shard_map/ppermute | solution.py:31
  98.4 13.8 %collective-permute-start.22 = (bf16[4,16,2304]{2,1,0:T(8,128)(2,1)S(1)}, bf16[4,16,2304]{2,1,0:T(8,128)(2,1)S(1)}, u32[]{:S(2)}, u32[]{:S(2)}) collective-permute-start(bf16[4,16,2304]{2,1,0:T(8,128)(2,1)S(1)} %get-tuple-element.28), channel_id=1, source_target_pairs={{0,68},{1,69},{2,70},{3,71},{4,64},{5,65},{6,66},{7,67},{8,12},{9,... | collective-permute-start | bytes 884744 | tf_op jit(solution)/shard_map/ppermute | solution.py:31
  100.9 8.0 %collective-permute-start.18 = (bf16[2,2,16,2304]{3,2,0,1:T(8,128)(2,1)S(1)}, bf16[2,2,16,2304]{3,2,0,1:T(8,128)(2,1)S(1)}, u32[]{:S(2)}, u32[]{:S(2)}) collective-permute-start(bf16[2,2,16,2304]{3,2,0,1:T(8,128)(2,1)S(1)} %copy.18), channel_id=1, source_target_pairs={{0,48},{1,49},{2,50},{3,51},{4,52},{5,53},{6,54},{7,55},{8,24},{9,... | collective-permute-start | bytes 884744 | tf_op jit(solution)/shard_map/ppermute | solution.py:31
  101.9 10.1 %collective-permute-start.16 = (bf16[2,2,16,2304]{3,2,0,1:T(8,128)(2,1)S(1)}, bf16[2,2,16,2304]{3,2,0,1:T(8,128)(2,1)S(1)}, u32[]{:S(2)}, u32[]{:S(2)}) collective-permute-start(bf16[2,2,16,2304]{3,2,0,1:T(8,128)(2,1)S(1)} %copy.16), channel_id=1, source_target_pairs={{0,48},{1,49},{2,50},{3,51},{4,52},{5,53},{6,54},{7,55},{8,24},{9,... | collective-permute-start | bytes 884744 | tf_op jit(solution)/shard_map/ppermute | solution.py:31
  105.3 6.9 %collective-permute-start.24 = (bf16[4,16,2304]{2,1,0:T(8,128)(2,1)S(1)}, bf16[4,16,2304]{2,1,0:T(8,128)(2,1)S(1)}, u32[]{:S(2)}, u32[]{:S(2)}) collective-permute-start(bf16[4,16,2304]{2,1,0:T(8,128)(2,1)S(1)} %add_convert_fusion.1), channel_id=1, source_target_pairs={{0,4},{1,5},{2,6},{3,7},{4,0},{5,1},{6,2},{7,3},{8,76},{9,77},{10,... | collective-permute-start | bytes 884744 | tf_op jit(solution)/shard_map/ppermute | solution.py:31
  112.2 6.8 %collective-permute-start.19 = (bf16[4,16,2304]{2,1,0:T(8,128)(2,1)S(1)}, bf16[4,16,2304]{2,1,0:T(8,128)(2,1)S(1)}, u32[]{:S(2)}, u32[]{:S(2)}) collective-permute-start(bf16[4,16,2304]{2,1,0:T(8,128)(2,1)S(1)} %pad_maximum_fusion), channel_id=1, source_target_pairs={{0,16},{1,17},{2,18},{3,19},{4,20},{5,21},{6,22},{7,23},{8,56},{9,... | collective-permute-start | bytes 884744 | tf_op jit(solution)/shard_map/ppermute | solution.py:31
  112.4 7.8 %collective-permute-start.25 = (bf16[2,16,2304]{2,1,0:T(8,128)(2,1)S(1)}, bf16[2,16,2304]{2,1,0:T(8,128)(2,1)S(1)}, u32[]{:S(2)}, u32[]{:S(2)}) collective-permute-start(bf16[2,16,2304]{2,1,0:T(8,128)(2,1)S(1)} %slice.127), channel_id=1, source_target_pairs={{0,48},{1,49},{2,50},{3,51},{4,52},{5,53},{6,54},{7,55},{8,24},{9,... | collective-permute-start | bytes 442376 | tf_op jit(solution)/shard_map/ppermute | solution.py:31
  119.2 6.6 %collective-permute-start.20 = (bf16[2,16,2304]{2,1,0:T(8,128)(2,1)S(1)}, bf16[2,16,2304]{2,1,0:T(8,128)(2,1)S(1)}, u32[]{:S(2)}, u32[]{:S(2)}) collective-permute-start(bf16[2,16,2304]{2,1,0:T(8,128)(2,1)S(1)} %pad_maximum_fusion.1), channel_id=1, source_target_pairs={{0,68},{1,69},{2,70},{3,71},{4,64},{5,65},{6,66},{7,67},{8,12},{9,... | collective-permute-start | bytes 442376 | tf_op jit(solution)/shard_map/ppermute | solution.py:31
  120.2 5.6 %collective-permute-start.26 = (bf16[16,2304]{1,0:T(8,128)(2,1)S(1)}, bf16[16,2304]{1,0:T(8,128)(2,1)S(1)}, u32[]{:S(2)}, u32[]{:S(2)}) collective-permute-start(bf16[16,2304]{1,0:T(8,128)(2,1)S(1)} %slice_bitcast_fusion.4), channel_id=1, source_target_pairs={{0,16},{1,17},{2,18},{3,19},{4,20},{5,21},{6,22},{7,23},{8,56},{9,... | collective-permute-start | bytes 221192 | tf_op jit(solution)/shard_map/ppermute | solution.py:31
  125.8 4.4 %collective-permute-start.21 = (bf16[16,2304]{1,0:T(8,128)(2,1)S(1)}, bf16[16,2304]{1,0:T(8,128)(2,1)S(1)}, u32[]{:S(2)}, u32[]{:S(2)}) collective-permute-start(bf16[16,2304]{1,0:T(8,128)(2,1)S(1)} %fusion.5), channel_id=1, source_target_pairs={{0,4},{1,5},{2,6},{3,7},{4,0},{5,1},{6,2},{7,3},{8,76},{9,77},{10,... | collective-permute-start | bytes 221192 | tf_op jit(solution)/shard_map/ppermute | solution.py:31
  130.3 11.4 %collective-permute-start.27 = (bf16[32,1152]{1,0:T(8,128)(2,1)S(1)}, bf16[32,1152]{1,0:T(8,128)(2,1)S(1)}, u32[]{:S(2)}, u32[]{:S(2)}) collective-permute-start(bf16[32,1152]{1,0:T(8,128)(2,1)S(1)} %pad_maximum_fusion.2), channel_id=1, source_target_pairs={{0,3},{1,2},{2,1},{3,0},{4,7},{5,6},{6,5},{7,4},{8,9},{9,8},{10,11... | collective-permute-start | bytes 221192 | tf_op jit(solution)/shard_map/ppermute | solution.py:31
  141.8 4.1 %collective-permute-start.28 = (bf16[32,576]{1,0:T(8,128)(2,1)S(1)}, bf16[32,576]{1,0:T(8,128)(2,1)S(1)}, u32[]{:S(2)}, u32[]{:S(2)}) collective-permute-start(bf16[32,576]{1,0:T(8,128)(2,1)S(1)} %slice.133), channel_id=1, source_target_pairs={{0,1},{1,0},{2,3},{3,2},{4,5},{5,4},{6,7},{7,6},{8,11},{9,10},{10,... | collective-permute-start | bytes 110600 | tf_op jit(solution)/shard_map/ppermute | solution.py:31
  (34 other events, 303.3 us)
